TPU v7x, 32 devices: a whole 2x2x4 slice. The times are simulated.
32 devices in a mesh: req: 2 (over x), wide: 16 (over z, y, core).
Axes of the slice: x: 2, y: 2, z: 4, core: 2. Of those that a mesh axis runs over, the one named last changes fastest.
Arguments:
- tokens: bfloat16 [256, 7168], P(('req', 'wide')), may hold values from -6 to 6
- attn_gain: bfloat16 [7168], replicated, may hold values from 0.099609375 to 1.8984375
- qkv_weight: bfloat16 [7168, 3, 7168], P(None, None, 'wide'), may hold values from -0.122756126 to 0.122756126
- adapter_down: bfloat16 [7168, 384], P('wide'), may hold values from -0.0625 to 0.0625
- adapter_up: bfloat16 [3, 128, 7168], P(None, None, 'wide'), may hold values from -0.5 to 0.5
- out_weight: bfloat16 [7168, 3584], P('wide'), may hold values from -0.0625 to 0.0625
- mlp_gain: bfloat16 [3584], replicated, may hold values from 0.099609375 to 1.8984375
- gate_up: bfloat16 [2, 14336, 3584], P(None, ('req', 'wide')), may hold values from -0.09375 to 0.09375
- down_weight: bfloat16 [14336, 3584], P(('req', 'wide')), may hold values from -0.046875 to 0.046875
- key_cache: bfloat16 [2, 4096, 7168], P('req', 'wide'), may hold values from -12 to 12
- value_cache: bfloat16 [2, 4096, 7168], P('req', 'wide'), may hold values from -6 to 6
- cache_lengths: int32 [2], P('req'), may hold values from 65 to 4096, as said below
- slot_mask: int32 [2, 4096], P('req', 'wide'), may hold values 0 or 1
- span_counts: int32 [2], P('req'), may hold values from 32 to 128, as said below
Outputs:
- hidden_out: bfloat16 [256, 3584], P(('req', 'wide'))
- attention: bfloat16 [256, 7168], P('req', 'wide')
- new_keys: bfloat16 [256, 7168], P('req', 'wide')
- new_values: bfloat16 [256, 7168], P('req', 'wide')
Inputs may be any that keep to these rules, and one draw needn't show every extreme that they name: `cache_lengths`: the longest request has exactly 4096 filled positions in every draw. `span_counts`: some request fills all 128 slots in every draw.
All inputs are finite; a program needn't handle non-finite values. No bound on the sum of `slot_mask` on one device may be relied on, other than what follows from the above.
Results may differ from a plain program's by a relative error of at most 0.024.
Values may be sent and summed in bfloat16 or wider, within the bound.
A program may use at most 512 MiB of HBM per device.

v0:
```python
import jax
import jax.numpy as jnp
from jax import lax
from jax.sharding import PartitionSpec as P

D = 7168
HEADS = 32
HD = 224
RANK = 128
SPAN = 128


EPSILON = 1e-05
NEG_LARGE = -1e30


def joined_2(value, axis, join):
    pieces = jax.tree.map(lambda part: lax.all_gather(part, axis), value)
    head = jax.tree.map(lambda part: part[0], pieces)
    tail = jax.tree.map(lambda part: part[1:], pieces)
    so_far, _ = lax.scan(lambda so_far, slab: (join(so_far, slab), None), head, tail)
    return so_far


def rms_scale(values, gains):
    widened = values.astype(jnp.float32)
    meansq = jnp.mean(widened * widened, axis=-1, keepdims=True)
    return (widened * lax.rsqrt(meansq + EPSILON) * gains.astype(jnp.float32)).astype(jnp.bfloat16)


def softmax_join(first, second):
    first_num, first_max, first_sum = first
    second_num, second_max, second_sum = second
    highest = jnp.maximum(first_max, second_max)
    first_factor = jnp.exp(first_max - highest)
    second_factor = jnp.exp(second_max - highest)
    joined_num = first_num * first_factor[..., None] + second_num * second_factor[..., None]
    return (joined_num, highest, first_sum * first_factor + second_sum * second_factor)


def feed_forward(row_block, gate_rows, down_rows):
    both = jnp.einsum("td,cfd->ctf", row_block, gate_rows, preferred_element_type=jnp.float32)
    hidden = (jax.nn.silu(both[0]) * both[1]).astype(jnp.bfloat16)
    return jnp.dot(hidden, down_rows, preferred_element_type=jnp.float32)


def body(
    tokens,
    attn_gain,
    qkv_weight,
    adapter_down,
    adapter_up,
    out_weight,
    mlp_gain,
    gate_up,
    down_weight,
    key_cache,
    value_cache,
    cache_lengths,
    slot_mask,
    span_counts,
):
    score_scale = HD ** (-0.5)
    local_width = qkv_weight.shape[2]
    local_heads = local_width // HD
    wide_index = lax.axis_index("wide")
    feature_start = wide_index * local_width
    head_start = wide_index * local_heads
    normed = rms_scale(tokens, attn_gain)
    flat_weight = qkv_weight.reshape(D, 3 * local_width)
    shard_rows = lax.all_gather(normed, "wide", axis=0, tiled=True)
    base_part = jnp.dot(shard_rows, flat_weight, preferred_element_type=jnp.float32)
    sliced = lax.dynamic_slice_in_dim(shard_rows, feature_start, local_width, 1)
    partial_low = jnp.dot(sliced, adapter_down, preferred_element_type=jnp.float32)
    united_rows = jnp.concatenate([base_part, partial_low], axis=1)
    lowrank = lax.psum(united_rows[:, 3 * local_width :], "wide").astype(jnp.bfloat16)
    adapted = jnp.einsum(
        "tcr,crd->tcd",
        lowrank.reshape(SPAN, 3, RANK),
        adapter_up,
        preferred_element_type=jnp.float32,
    )
    projected = (united_rows[:, : 3 * local_width].reshape(SPAN, 3, local_width) + adapted).astype(
        jnp.bfloat16
    )
    query_own = projected[:, 0]
    new_keys = projected[:, 1]
    new_values = projected[:, 2]
    query_all = lax.all_gather(query_own, "wide", axis=1, tiled=True)
    block_len = key_cache.shape[1]
    block_start = wide_index * block_len
    length = cache_lengths[0]
    usable = (block_start + jnp.arange(block_len) < length) & (slot_mask[0] == 1)
    query_heads = query_all.reshape(SPAN, HEADS, HD)

    def cache_block(unused):
        key_heads = key_cache[0].reshape(block_len, HEADS, HD)
        value_heads = value_cache[0].reshape(block_len, HEADS, HD)
        scores = (
            jnp.einsum("qhd,khd->qhk", query_heads, key_heads, preferred_element_type=jnp.float32)
            * score_scale
        )
        scores = jnp.where(usable, scores, NEG_LARGE)
        highest = jnp.max(scores, axis=-1)
        weights = jnp.where(usable, jnp.exp(scores - highest[..., None]), 0.0)
        totals = jnp.sum(weights, axis=-1)
        numerator = jnp.einsum(
            "qhk,khd->qhd",
            weights.astype(jnp.bfloat16),
            value_heads,
            preferred_element_type=jnp.float32,
        )
        return (numerator, highest, totals)

    def skipped(unused):
        return (
            jnp.zeros((SPAN, HEADS, HD), jnp.float32),
            jnp.full((SPAN, HEADS), NEG_LARGE, jnp.float32),
            jnp.zeros((SPAN, HEADS), jnp.float32),
        )

    partial_value = lax.cond(block_start < length, cache_block, skipped, 0)
    span_count = span_counts[0]
    query_pos = jnp.arange(SPAN)[:, None]
    key_pos = jnp.arange(SPAN)[None, :]
    span_ok = ((key_pos <= query_pos) & ((key_pos < span_count) | (key_pos == query_pos)))[
        :, None, :
    ]
    own_query = query_own.reshape(SPAN, local_heads, HD)
    own_keys = new_keys.reshape(SPAN, local_heads, HD)
    own_values = new_values.reshape(SPAN, local_heads, HD)
    own_scores = (
        jnp.einsum("qhd,khd->qhk", own_query, own_keys, preferred_element_type=jnp.float32)
        * score_scale
    )
    own_scores = jnp.where(span_ok, own_scores, NEG_LARGE)
    own_max = jnp.max(own_scores, axis=-1)
    own_weights = jnp.where(span_ok, jnp.exp(own_scores - own_max[..., None]), 0.0)
    own_sum = jnp.sum(own_weights, axis=-1)
    own_num = jnp.einsum(
        "qhk,khd->qhd",
        own_weights.astype(jnp.bfloat16),
        own_values,
        preferred_element_type=jnp.float32,
    )
    sliced_part = tuple(
        (lax.dynamic_slice_in_dim(member, head_start, local_heads, 1) for member in partial_value)
    )
    joined = softmax_join(sliced_part, (own_num, own_max, own_sum))
    partial_value = tuple(
        (
            lax.dynamic_update_slice_in_dim(member, update, head_start, 1)
            for member, update in zip(partial_value, joined)
        )
    )

    def flat_join(first, second):
        first_heads = (first[0].reshape(SPAN, HEADS, HD), first[1], first[2])
        second_heads = (second[0].reshape(SPAN, HEADS, HD), second[1], second[2])
        joined_all = softmax_join(first_heads, second_heads)
        return (joined_all[0].reshape(SPAN, D), joined_all[1], joined_all[2])

    merged = joined_2(
        (partial_value[0].reshape(SPAN, D), partial_value[1], partial_value[2]), "wide", flat_join
    )
    numerator = lax.dynamic_slice_in_dim(merged[0], feature_start, local_width, 1).reshape(
        SPAN, local_heads, HD
    )
    totals = lax.dynamic_slice_in_dim(merged[2], head_start, local_heads, 1)
    attention = (numerator / totals[..., None]).reshape(SPAN, local_width).astype(jnp.bfloat16)
    attn_out = lax.psum_scatter(
        jnp.dot(attention, out_weight, preferred_element_type=jnp.float32),
        "wide",
        scatter_dimension=0,
        tiled=True,
    )
    normed_mid = rms_scale(attn_out, mlp_gain)
    every_row = lax.all_gather(normed_mid, ("req", "wide"), axis=0, tiled=True)
    mlp_out = lax.psum_scatter(
        feed_forward(every_row, gate_up, down_weight),
        ("req", "wide"),
        scatter_dimension=0,
        tiled=True,
    )
    hidden_out = mlp_out.astype(jnp.bfloat16)
    return (hidden_out, attention, new_keys, new_values)


def solution(mesh):
    return jax.shard_map(
        body,
        mesh=mesh,
        in_specs=(
            P(("req", "wide"), None),
            P(),
            P(None, None, "wide"),
            P("wide", None),
            P(None, None, "wide"),
            P("wide", None),
            P(),
            P(None, ("req", "wide"), None),
            P(("req", "wide"), None),
            P("req", "wide", None),
            P("req", "wide", None),
            P("req"),
            P("req", "wide"),
            P("req"),
        ),
        out_specs=(P(("req", "wide"), None), P("req", "wide"), P("req", "wide"), P("req", "wide")),
        check_vma=False,
    )
```

profile of v0, /device:TPU:0, one launch (start us, length us, event | category | flops | bytes accessed | tf_op | source)
XLA Modules:
  0.0 1049.5 jit_solution(4112117198588744390)
XLA Ops:
  11.0 43.4 %all-gather.6.cloned.1.call-done = bf16[128,7168]{1,0:T(8,128)(2,1)} async-done(((bf16[8,7168]{1,0:T(8,128)(2,1)}), bf16[128,7168]{1,0:T(8,128)(2,1)}) %all-gather.6.cloned.1.call-update) | async-done | bytes 1835024 | tf_op jit(solution)/shard_map/all_gather | solution.py:71
  55.7 60.9 %all-reduce.1 = bf16[128,384]{1,0:T(8,128)(2,1)S(1)} all-reduce(f32[128,384]{1,0:T(8,128)S(1)} %fusion.45), channel_id=1, replica_groups=mesh['req'=2,'wide'=16] {'wide'}, use_global_device_ids=true, to_apply=%region_1.0 | all-reduce | flops 49152 | bytes 294912 | tf_op jit(solution)/shard_map/psum | solution.py:76
  116.8 9.7 fusion.21
  130.3 35.3 %all-gather.12.cloned.1.call-done = bf16[128,1,7168]{0,2,1:T(8,128)(2,1)} async-done(((bf16[128,1,448]{0,2,1:T(8,128)(2,1)}), bf16[128,1,7168]{0,2,1:T(8,128)(2,1)}) %all-gather.12.cloned.1.call-update) | async-done | bytes 1835024 | tf_op jit(solution)/shard_map/all_gather | solution.py:89
  165.6 28.7 %conditional.1 = (f32[128,32,224]{0,2,1:T(8,128)}, f32[128,32]{0,1:T(8,128)}, f32[128,32]{0,1:T(8,128)}, f32[1,128,32]{1,2,0:T(8,128)S(1)}, f32[1,128,32]{1,2,0:T(8,128)S(1)}) conditional(s32[]{:T(128)} %convert_element_type.39, () %tuple.24, (s32[]{:T(128)}, bf16[1,256,7168]{2,1,0:T(8,128)(2,1)}, bf16[128,7168]{0,1:T(8,128)(2,1)}, ...), branch_computations={%region_2.0_spmd, %region_3.6_spmd.clone} | conditional | flops 953148416 | bytes 57085544 | solution.py:122
  166.3 5.9 copy.48
  180.8 5.9 copy.49
  186.7 6.8 fusion.15
  196.8 5.3 copy.51
  202.2 20.6 %all_gather.36 = f32[16,128,32]{1,2,0:T(8,128)S(1)} all-gather(f32[1,128,32]{1,2,0:T(8,128)S(1)} %get-tuple-element.157), channel_id=1, replica_groups=mesh['req'=2,'wide'=16] {'wide'}, dimensions={0}, use_global_device_ids=true | all-gather | bytes 278528 | tf_op jit(solution)/shard_map/all_gather | solution.py:18
  222.8 19.6 %all_gather.38 = f32[16,128,32]{1,2,0:T(8,128)S(1)} all-gather(f32[1,128,32]{1,2,0:T(8,128)S(1)} %get-tuple-element.147), channel_id=1, replica_groups=mesh['req'=2,'wide'=16] {'wide'}, dimensions={0}, use_global_device_ids=true | all-gather | bytes 278528 | tf_op jit(solution)/shard_map/all_gather | solution.py:18
  243.1 247.3 %all-gather.8.cloned.1.call-done = f32[16,128,7168]{2,1,0:T(8,128)} async-done(((f32[1,128,7168]{2,1,0:T(8,128)}), f32[16,128,7168]{2,1,0:T(8,128)}) %all-gather.8.cloned.1.call-update) | async-done | bytes 58720272 | tf_op jit(solution)/shard_map/all_gather | solution.py:18
  499.8 37.2 %slice.51 = f32[15,128,7168]{2,1,0:T(8,128)} slice(f32[16,128,7168]{2,1,0:T(8,128)} %all-gather.8.cloned.1.call-done), slice={[1:16], [0:128], [0:7168]} | slice | bytes 110100480 | tf_op jit(solution)/shard_map/slice | solution.py:20
  537.0 233.2 %while.14 = (s32[]{:T(128)}, f32[128,7168]{0,1:T(8,128)}, f32[128,32]{0,1:T(8,128)S(1)}, f32[128,32]{0,1:T(8,128)S(1)}, f32[15,128,32]{1,2,0:T(8,128)S(1)}, /*in...) while((s32[]{:T(128)}, f32[128,7168]{0,1:T(8,128)}, f32[128,32]{0,1:T(8,128)S(1)}, ...), condition=%wide.region_9.10_spmd, body=%wide.region_8.9_spmd.sunk | while | flops 2777090 | bytes 25854044 | solution.py:21
  547.3 5.3 fusion.80
  562.8 5.3 fusion.80
  578.4 5.3 fusion.80
  593.9 5.3 fusion.80
  609.5 5.3 fusion.80
  625.0 5.3 fusion.80
  640.5 5.3 fusion.80
  656.1 5.3 fusion.80
  671.6 5.3 fusion.80
  687.2 5.3 fusion.80
  702.7 5.3 fusion.80
  718.3 5.3 fusion.80
  733.8 5.3 fusion.80
  749.4 5.3 fusion.80
  764.9 5.3 fusion.80
  775.2 60.5 %reduce-scatter.3.cloned.1.call-done = f32[8,3584]{1,0:T(8,128)} async-done(((f32[128,3584]{1,0:T(8,128)}), f32[8,3584]{1,0:T(8,128)}) %reduce-scatter.3.cloned.1.call-update) | async-done | bytes 114704 | tf_op jit(solution)/shard_map/reduce_scatter | solution.py:171
  838.4 55.4 %all-gather.10.cloned.1.call-done = bf16[256,3584]{1,0:T(8,128)(2,1)} async-done(((bf16[8,3584]{1,0:T(8,128)(2,1)}), bf16[256,3584]{1,0:T(8,128)(2,1)}) %all-gather.10.cloned.1.call-update) | async-done | bytes 1835024 | tf_op jit(solution)/shard_map/all_gather | solution.py:178
  902.0 139.1 %reduce-scatter.5.cloned.1.call-done = f32[8,3584]{1,0:T(8,128)} async-done(((f32[256,3584]{1,0:T(8,128)}), f32[8,3584]{1,0:T(8,128)}) %reduce-scatter.5.cloned.1.call-update) | async-done | bytes 114704 | tf_op jit(solution)/shard_map/reduce_scatter | solution.py:179
  (111 shorter events, 201.2 us)
Async XLA Ops:
  7.2 891.8 %copy-start = (bf16[448,3584]{1,0:T(8,128)(2,1)S(1)}, bf16[448,3584]{1,0:T(8,128)(2,1)}, u32[]{:S(2)}) copy-start(bf16[448,3584]{1,0:T(8,128)(2,1)} %param.26) | copy-start | bytes 9633796
  7.2 47.2 %all-gather.6.cloned.1.call-start = ((), (), s32[]{:S(2)}) async-start(), calls=%async_computation.2 | async-start | bytes 1949696 | tf_op jit(solution)/shard_map/all_gather | solution.py:71
  10.9 154.7 %all-gather.12.cloned.1.call-start = ((), (), s32[]{:S(2)}) async-start(), calls=%async_computation.7 | async-start | bytes 1949696 | tf_op jit(solution)/shard_map/all_gather | solution.py:89
  116.8 9.8 copy-start.4
  116.8 48.8 %copy-start.7 = (s32[1,256]{1,0:T(1,128)S(1)}, s32[1,256]{1,0:T(1,128)}, u32[]{:S(2)}) copy-start(s32[1,256]{1,0:T(1,128)} %param.30) | copy-start | bytes 3076
  127.6 362.8 %all-gather.8.cloned.1.call-start = ((), (), s32[]{:S(2)}) async-start(), calls=%async_computation.3 | async-start | bytes 62390272 | tf_op jit(solution)/shard_map/all_gather | solution.py:18
  177.0 1.9 copy-start.1
  180.8 5.9 copy-start.5
  202.1 633.5 %reduce-scatter.3.cloned.1.call-start = ((), (), s32[]{:S(2)}) async-start(), calls=%async_computation.4 | async-start | bytes 1949696 | tf_op jit(solution)/shard_map/reduce_scatter | solution.py:171
  222.8 271.8 %copy-start.2 = (f32[16,128,32]{1,2,0:T(8,128)}, f32[16,128,32]{1,2,0:T(8,128)S(1)}, u32[]{:S(2)}) copy-start(f32[16,128,32]{1,2,0:T(8,128)S(1)} %all_gather.36) | copy-start | bytes 786436
  499.8 37.2 %slice-start = ((f32[16,128,32]{1,2,0:T(8,128)}), f32[15,128,32]{1,2,0:T(8,128)S(1)}, s32[]{:S(2)}) async-start(f32[16,128,32]{1,2,0:T(8,128)} %copy-done.2), calls=%async_computation.8 | async-start | bytes 491520 | tf_op jit(solution)/shard_map/slice | solution.py:20
  770.2 4.9 copy-start.6
  771.2 67.1 %copy-start.3 = (bf16[128,448]{0,1:T(8,128)(2,1)}, bf16[128,448]{0,1:T(8,128)(2,1)S(1)}, u32[]{:S(2)}) copy-start(bf16[128,448]{0,1:T(8,128)(2,1)S(1)} %fusion.43) | copy-start | bytes 344068
  775.1 118.6 %all-gather.10.cloned.1.call-start = ((), (), s32[]{:S(2)}) async-start(), calls=%async_computation.5 | async-start | bytes 1892352 | tf_op jit(solution)/shard_map/all_gather | solution.py:178
  838.3 202.7 %reduce-scatter.5.cloned.1.call-start = ((), (), s32[]{:S(2)}) async-start(), calls=%async_computation.6 | async-start | bytes 3784704 | tf_op jit(solution)/shard_map/reduce_scatter | solution.py:179
Sparse Core Ops, SparseCore 0:
  11.0 43.3 all-gather.5
  127.7 37.8 all-gather.11
  202.3 288.1 all-gather.7
  775.2 60.3 reduce-scatter.2
  839.0 54.7 all-gather.9
  902.1 138.9 reduce-scatter.4
where the time goes:
time: 1050 us
  waiting for transfers between devices  581 us (55%)
  local copies, waits for them, and re-layouts  210 us (20%)
  other arithmetic  103 us (10%)
  blocking collectives  101 us (10%)
  matrix products  38 us (4%)
  between operations  15.6 us (1%)
    all_gather x1, waiting for transfers between devices, joined_2(): pieces = jax.tree.map(lambda part: lax.all_gather(part, axis), value)  247 us
    dynamic_slice x30, local copies, waits for them, and re-layouts, joined_2(): lax.scan(lambda so_far, slab: (join(so_far, slab), None), head, tail)  142 us
    reduce_scatter x1, waiting for transfers between devices, body(): lax.psum_scatter(feed_forward(every_row, gate_up, down_weight), ('req', '...  139 us
    add x15, other arithmetic, softmax_join(): first_num * first_factor[..., None] + second_num * second_factor[..., None]  79.7 us
    psum x1, blocking collectives, body(): lax.psum(united_rows[:, 3 * local_width:], 'wide').astype(jnp.bfloat16)  60.9 us
    reduce_scatter x1, waiting for transfers between devices, body(): lax.psum_scatter(jnp.dot(attention, out_weight, preferred_element_type=jn...  60.5 us
    all_gather x1, waiting for transfers between devices, body(): every_row = lax.all_gather(normed_mid, ('req', 'wide'), axis=0, tiled=True)  55.4 us
    all_gather x1, waiting for transfers between devices, body(): shard_rows = lax.all_gather(normed, 'wide', axis=0, tiled=True)  43.4 us
  transfers between devices with their start and end apart: 6, of which 6 were waited for; matrix products, arithmetic and copies ran while one was open for 0% of the time, Pallas kernels for 0%

commit v1 on v0

v1 whole, which is shorter than its diff:
```python
import functools

import jax
import jax.numpy as jnp
from jax import lax
from jax.experimental import pallas as pl
from jax.experimental.pallas import tpu as pltpu
from jax.sharding import PartitionSpec as P

D = 7168
HEADS = 32
HD = 224
RANK = 128
SPAN = 128
GROUP = 4

EPSILON = 1e-05
NEG_LARGE = -1e30
MESH = pl.DeviceIdType.MESH
VMEM_LIMIT = 48 * 1024 * 1024


def rms_scale(values, gains):
    widened = values.astype(jnp.float32)
    meansq = jnp.mean(widened * widened, axis=-1, keepdims=True)
    return (widened * lax.rsqrt(meansq + EPSILON) * gains.astype(jnp.float32)).astype(jnp.bfloat16)


def params(collective_id=None):
    if collective_id is None:
        return pltpu.CompilerParams(vmem_limit_bytes=VMEM_LIMIT)
    return pltpu.CompilerParams(
        collective_id=collective_id, has_side_effects=True, vmem_limit_bytes=VMEM_LIMIT
    )


class Grid:
    def __init__(self, reqs, wide):
        self.wide = wide
        chips = wide // 2
        first = 4 if chips % 4 == 0 else 1
        self.size = dict(r=reqs, a=first, b=chips // first, c=2)

    def place(self):
        me = lax.axis_index("wide")
        b = self.size["b"]
        return dict(
            r=lax.axis_index("req"), a=me // (2 * b), b=(me // 2) % b, c=me % 2
        )

    def moved(self, place, **steps):
        out = dict(place)
        for axis, step in steps.items():
            if step:
                out[axis] = (place[axis] + step) % self.size[axis]
        return out

    def on_wide(self, place):
        return (place["a"] * self.size["b"] + place["b"]) * 2 + place["c"]

    def device(self, place):
        return (place["r"], self.on_wide(place))

    def barrier(self, me, axes):
        sem = pltpu.get_barrier_semaphore()
        count = 0
        for axis in axes:
            for step in range(1, self.size[axis]):
                pl.semaphore_signal(
                    sem,
                    inc=1,
                    device_id=self.device(self.moved(me, **{axis: step})),
                    device_id_type=MESH,
                )
                count += 1
        pl.semaphore_wait(sem, count)


def remote(src, dst, send, recv, device):
    return pltpu.make_async_remote_copy(
        src_ref=src, dst_ref=dst, send_sem=send, recv_sem=recv, device_id=device, device_id_type=MESH
    )


def spread(grid, me, order, x_ref, o_ref, send, recv, local):
    def slot(place):
        at = grid.on_wide(place)
        return place["r"] * grid.wide + at if "r" in order else at

    own = pltpu.make_async_copy(x_ref, o_ref.at[slot(me)], local)
    own.start()
    items = [((0,) * len(order), -1)]
    for k, axis in enumerate(order):
        items += [
            (steps[:k] + (s,) + steps[k + 1 :], k)
            for steps, _ in list(items)
            for s in range(1, grid.size[axis])
        ]
    items.sort(key=lambda item: (sum(1 for s in item[0] if s), item[1]))
    sends = []
    for steps, stage in items:
        place = grid.moved(me, **dict(zip(order, steps)))
        here = o_ref.at[slot(place)]
        if stage >= 0:
            remote(x_ref, here, send.at[0], recv.at[slot(place)], grid.device(me)).wait_recv()
        source = here if stage >= 0 else x_ref
        for k in range(stage + 1, len(order)):
            for s in range(1, grid.size[order[k]]):
                copy = remote(
                    source,
                    here,
                    send.at[len(sends)],
                    recv.at[slot(place)],
                    grid.device(grid.moved(me, **{order[k]: s})),
                )
                copy.start()
                sends.append(copy)
    own.wait()
    for copy in sends:
        copy.wait_send()


def gather_kernel(grid, order, x_ref, o_ref, send, recv, local):
    me = grid.place()
    grid.barrier(me, order)
    spread(grid, me, order, x_ref, o_ref, send, recv, local)


def gather(grid, order, x, collective_id):
    slots = grid.wide * (grid.size["r"] if "r" in order else 1)
    return pl.pallas_call(
        functools.partial(gather_kernel, grid, order),
        out_shape=jax.ShapeDtypeStruct((slots,) + x.shape, x.dtype),
        in_specs=[pl.BlockSpec(memory_space=pltpu.VMEM)],
        out_specs=pl.BlockSpec(memory_space=pltpu.VMEM),
        scratch_shapes=[
            pltpu.SemaphoreType.DMA((slots,)),
            pltpu.SemaphoreType.DMA((slots,)),
            pltpu.SemaphoreType.DMA,
        ],
        compiler_params=params(collective_id),
        name="gather" + str(collective_id),
    )(x)


def lowrank_kernel(grid, p_ref, o_ref, r_ref, t_ref, sems):
    me = lax.axis_index("wide")
    req = lax.axis_index("req")
    n = grid.wide
    barrier = pltpu.get_barrier_semaphore()
    for d in range(1, n):
        pl.semaphore_signal(barrier, inc=1, device_id=(req, (me + d) % n), device_id_type=MESH)
    pl.semaphore_wait(barrier, n - 1)
    first = []
    for d in range(1, n):
        to = (me + d) % n
        copy = remote(p_ref.at[to], r_ref.at[d - 1], sems.at[0, d], sems.at[1, d], (req, to))
        copy.start()
        first.append(copy)
    total = p_ref[me]
    for d, copy in enumerate(first):
        copy.wait_recv()
        total = total + r_ref[d]
    t_ref[...] = total.astype(t_ref.dtype)
    second = []
    for d in range(1, n):
        copy = remote(t_ref, o_ref.at[me], sems.at[2, d], sems.at[3, d], (req, (me + d) % n))
        copy.start()
        second.append(copy)
    o_ref[me] = t_ref[...]
    for d in range(1, n):
        remote(t_ref, o_ref.at[(me + n - d) % n], sems.at[2, d], sems.at[3, d], (req, me)).wait_recv()
    for copy in first + second:
        copy.wait_send()


def lowrank_sum(grid, partial, collective_id):
    n, rows, width = partial.shape
    vmem = pl.BlockSpec(memory_space=pltpu.VMEM)
    return pl.pallas_call(
        functools.partial(lowrank_kernel, grid),
        out_shape=jax.ShapeDtypeStruct(partial.shape, jnp.bfloat16),
        in_specs=[vmem],
        out_specs=vmem,
        scratch_shapes=[
            pltpu.VMEM((n - 1, rows, width), jnp.float32),
            pltpu.VMEM((rows, width), jnp.bfloat16),
            pltpu.SemaphoreType.DMA((4, n)),
        ],
        compiler_params=params(collective_id),
        name="lowrank_sum",
    )(partial)


def add_join(first, second):
    return [x + y for x, y in zip(first, second)]


def softmax_join(first, second):
    num1, st1 = first
    num2, st2 = second
    max1, sum1 = st1[..., :GROUP, :], st1[..., GROUP:, :]
    max2, sum2 = st2[..., :GROUP, :], st2[..., GROUP:, :]
    highest = jnp.maximum(max1, max2)
    f1 = jnp.exp(max1 - highest)
    f2 = jnp.exp(max2 - highest)
    heads = num1.shape[-3]
    num = jnp.stack(
        [
            num1[..., i, :, :] * f1[..., i : i + 1, :] + num2[..., i, :, :] * f2[..., i : i + 1, :]
            for i in range(heads)
        ],
        axis=-3,
    )
    return [num, jnp.concatenate([highest, sum1 * f1 + sum2 * f2], axis=-2)]


def combine_down(grid, me, reqs, join, ps, sc, sems):
    R, A, B = reqs, grid.size["a"], grid.size["b"]
    r, a, b, c = (me["r"] if R > 1 else 0), me["a"], me["b"], me["c"]
    parts = range(len(ps))
    sends = []
    count = [0]

    def push(pairs, device):
        out = []
        for i, (src, dst) in enumerate(pairs):
            k = count[0]
            count[0] += 1
            copy = remote(src, dst, sems.at[0, k], sems.at[1, k], device)
            copy.start()
            out.append(copy)
        sends.extend(out)
        return out

    def arrived(copies):
        for copy in copies:
            copy.wait_recv()

    def wide_values(refs):
        return [ref[...].astype(jnp.float32) for ref in refs]

    others = list(range(1, B)) + [0]
    core = {}
    peer = grid.device(grid.moved(me, c=1))
    for dr in list(range(1, R)) + [0]:
        rr = (r + dr) % R if dr else r
        for db in others:
            bb = (b + db) % B if db else b
            core[dr, db] = push(
                [(ps[i].at[rr, :, bb, 1 - c], sc["r1"][i].at[rr, bb]) for i in parts], peer
            )
    along_r = {}
    for dr in range(1, R):
        rr = (r + dr) % R
        for db in others:
            bb = (b + db) % B if db else b
            arrived(core[dr, db])
            both = join(
                wide_values([ps[i].at[rr, :, bb, c] for i in parts]),
                wide_values([sc["r1"][i].at[rr, bb] for i in parts]),
            )
            for i in parts:
                sc["t1"][i][rr, bb] = both[i].astype(sc["t1"][i].dtype)
            along_r[dr, db] = push(
                [(sc["t1"][i].at[rr, bb], sc["r2"][i].at[dr - 1, bb]) for i in parts],
                grid.device(grid.moved(me, r=dr)),
            )
    along_b = {}
    for db in others:
        bb = (b + db) % B if db else b
        arrived(core[0, db])
        both = join(
            wide_values([ps[i].at[r, :, bb, c] for i in parts]),
            wide_values([sc["r1"][i].at[r, bb] for i in parts]),
        )
        for dr in range(1, R):
            arrived(along_r[dr, db])
            both = join(both, wide_values([sc["r2"][i].at[dr - 1, bb] for i in parts]))
        if db:
            for i in parts:
                sc["t2"][i][bb] = both[i].astype(sc["t2"][i].dtype)
            along_b[db] = push(
                [(sc["t2"][i].at[bb], sc["r3"][i].at[db - 1]) for i in parts],
                grid.device(grid.moved(me, b=db)),
            )
    for db in range(1, B):
        arrived(along_b[db])
        both = join(both, wide_values([sc["r3"][i].at[db - 1] for i in parts]))
    for i in parts:
        sc["own"][i][...] = both[i]
        sc["t3"][i][...] = both[i].astype(sc["t3"][i].dtype)
    along_a = []
    for da in range(1, A):
        aa = (a + da) % A
        along_a.append(
            push(
                [(sc["t3"][i].at[aa], sc["r4"][i].at[da - 1]) for i in parts],
                grid.device(grid.moved(me, a=da)),
            )
        )
    total = [sc["own"][i][a] for i in parts]
    for da in range(1, A):
        arrived(along_a[da - 1])
        total = join(total, wide_values([sc["r4"][i].at[da - 1] for i in parts]))
    return total, sends


SCRATCH = ("r1", "t1", "r2", "t2", "r3", "own", "t3", "r4")


def reduce_scratch(grid, reqs, slabs):
    R, A, B = reqs, grid.size["a"], grid.size["b"]
    lead = dict(
        r1=(R, B, A),
        t1=(R if R > 1 else 1, B if R > 1 else 1, A if R > 1 else 1),
        r2=(R - 1, B, A) if R > 1 else (1, 1, 1),
        t2=(B, A),
        r3=(max(B - 1, 1), A),
        own=(A,),
        t3=(A,),
        r4=(max(A - 1, 1),),
    )
    shapes = []
    for name in SCRATCH:
        for shape, dtype in slabs:
            shapes.append(
                pltpu.VMEM(lead[name] + tuple(shape), jnp.float32 if name == "own" else dtype)
            )
    copies = (R * B + (R - 1) * B + (B - 1) + (A - 1)) * len(slabs)
    shapes.append(pltpu.SemaphoreType.DMA((2, copies)))
    return shapes


def reduce_kernel(grid, reqs, join, parts, *refs):
    ps, outs, rest, sems = refs[:parts], refs[parts : 2 * parts], refs[2 * parts : -1], refs[-1]
    sc = {name: rest[k * parts : (k + 1) * parts] for k, name in enumerate(SCRATCH)}
    me = grid.place()
    grid.barrier(me, ("r", "a", "b", "c") if reqs > 1 else ("a", "b", "c"))
    total, sends = combine_down(grid, me, reqs, join, ps, sc, sems)
    for out, value in zip(outs, total):
        out[...] = value.astype(out.dtype)
    for copy in sends:
        copy.wait_send()


def reduce_scatter(grid, reqs, join, arrays, out_dtypes, collective_id):
    A, B = grid.size["a"], grid.size["b"]
    slabs = [(x.shape[1:], x.dtype) for x in arrays]
    vmem = pl.BlockSpec(memory_space=pltpu.VMEM)
    return pl.pallas_call(
        functools.partial(reduce_kernel, grid, reqs, join, len(arrays)),
        out_shape=[jax.ShapeDtypeStruct(s, t) for (s, _), t in zip(slabs, out_dtypes)],
        in_specs=[vmem] * len(arrays),
        out_specs=[vmem] * len(arrays),
        scratch_shapes=reduce_scratch(grid, reqs, slabs),
        compiler_params=params(collective_id),
        name="reduce" + str(collective_id),
    )(*[x.reshape((reqs, A, B, 2) + x.shape[1:]) for x in arrays])


def cache_kernel(heads, q_ref, k_ref, v_ref, ok_ref, num_ref, st_ref):
    ok = ok_ref[...] > 0.0
    st_ref[...] = jnp.zeros_like(st_ref)
    for i in range(GROUP):
        keys = k_ref[0, :, i * HD : (i + 1) * HD]
        values = v_ref[0, :, i * HD : (i + 1) * HD]
        scores = jnp.dot(keys, q_ref[i], preferred_element_type=jnp.float32) * HD ** (-0.5)
        scores = jnp.where(ok, scores, NEG_LARGE)
        highest = jnp.max(scores, axis=0, keepdims=True)
        weights = jnp.where(ok, jnp.exp(scores - highest), 0.0)
        num = lax.dot_general(
            values,
            weights.astype(jnp.bfloat16),
            (((0,), (0,)), ((), ())),
            preferred_element_type=jnp.float32,
        )
        num_ref[i] = num.astype(jnp.bfloat16)
        slab, row = i // heads, i % heads
        st_ref[slab, row : row + 1, :] = highest
        st_ref[slab, GROUP + row : GROUP + row + 1, :] = jnp.sum(weights, axis=0, keepdims=True)


def cache_attention(heads, query, keys, values, usable):
    block = keys.shape[1]
    cols = GROUP * HD
    kv = pl.BlockSpec((1, block, cols), lambda i: (0, 0, i))
    return pl.pallas_call(
        functools.partial(cache_kernel, heads),
        grid=(HEADS // GROUP,),
        in_specs=[
            pl.BlockSpec((GROUP, HD, SPAN), lambda i: (i, 0, 0)),
            kv,
            kv,
            pl.BlockSpec((block, SPAN), lambda i: (0, 0)),
        ],
        out_specs=[
            pl.BlockSpec((GROUP, HD, SPAN), lambda i: (i, 0, 0)),
            pl.BlockSpec((GROUP // heads, 2 * GROUP, SPAN), lambda i: (i, 0, 0)),
        ],
        out_shape=[
            jax.ShapeDtypeStruct((HEADS, HD, SPAN), jnp.bfloat16),
            jax.ShapeDtypeStruct((HEADS // heads, 2 * GROUP, SPAN), jnp.float32),
        ],
        compiler_params=params(),
        name="cache_attention",
    )(query, keys, values, usable)


def body(
    grid,
    tokens,
    attn_gain,
    qkv_weight,
    adapter_down,
    adapter_up,
    out_weight,
    mlp_gain,
    gate_up,
    down_weight,
    key_cache,
    value_cache,
    cache_lengths,
    slot_mask,
    span_counts,
):
    reqs, wide = grid.size["r"], grid.wide
    rows = tokens.shape[0]
    width = qkv_weight.shape[2]
    heads = width // HD
    wide_index = lax.axis_index("wide")
    normed = rms_scale(tokens, attn_gain)
    shard_rows = gather(grid, ("a", "b", "c"), normed, 0).reshape(SPAN, D)
    sliced = lax.dynamic_slice_in_dim(shard_rows, wide_index * width, width, 1)
    partial_low = jnp.dot(sliced, adapter_down, preferred_element_type=jnp.float32)
    lowrank = lowrank_sum(grid, partial_low.reshape(wide, rows, 3 * RANK), 1)
    base = jnp.dot(shard_rows, qkv_weight.reshape(D, 3 * width), preferred_element_type=jnp.float32)
    adapted = jnp.einsum(
        "tcr,crd->tcd",
        lowrank.reshape(SPAN, 3, RANK),
        adapter_up,
        preferred_element_type=jnp.float32,
    )
    projected = (base.reshape(SPAN, 3, width) + adapted).astype(jnp.bfloat16)
    query_own = projected[:, 0]
    new_keys = projected[:, 1]
    new_values = projected[:, 2]
    query_turned = query_own.T.reshape(heads, HD, SPAN)
    query_all = gather(grid, ("a", "b", "c"), query_turned, 2).reshape(HEADS, HD, SPAN)

    block_len = key_cache.shape[1]
    positions = wide_index * block_len + jnp.arange(block_len)
    usable = ((positions < cache_lengths[0]) & (slot_mask[0] == 1)).astype(jnp.float32)
    usable = jnp.broadcast_to(usable[:, None], (block_len, SPAN))
    num, stats = cache_attention(heads, query_all, key_cache, value_cache, usable)
    cache_num, cache_stats = reduce_scatter(
        grid,
        1,
        softmax_join,
        [num.reshape(wide, heads, HD, SPAN), stats],
        [jnp.float32, jnp.float32],
        3,
    )

    span_count = span_counts[0]
    query_pos = jnp.arange(SPAN)[None, :]
    key_pos = jnp.arange(SPAN)[:, None]
    span_ok = (key_pos <= query_pos) & ((key_pos < span_count) | (key_pos == query_pos))
    own_scores = (
        jnp.einsum(
            "hdq,khd->hkq",
            query_turned,
            new_keys.reshape(SPAN, heads, HD),
            preferred_element_type=jnp.float32,
        )
        * HD ** (-0.5)
    )
    own_scores = jnp.where(span_ok, own_scores, NEG_LARGE)
    own_max = jnp.max(own_scores, axis=1)
    own_weights = jnp.where(span_ok, jnp.exp(own_scores - own_max[:, None]), 0.0)
    own_sum = jnp.sum(own_weights, axis=1)
    own_num = jnp.einsum(
        "hkq,khd->hdq",
        own_weights.astype(jnp.bfloat16),
        new_values.reshape(SPAN, heads, HD),
        preferred_element_type=jnp.float32,
    )
    cache_max, cache_sum = cache_stats[:heads], cache_stats[GROUP : GROUP + heads]
    highest = jnp.maximum(cache_max, own_max)
    cache_factor = jnp.exp(cache_max - highest)
    own_factor = jnp.exp(own_max - highest)
    totals = cache_sum * cache_factor + own_sum * own_factor
    mixed = cache_num * cache_factor[:, None] + own_num * own_factor[:, None]
    attention = (mixed / totals[:, None]).astype(jnp.bfloat16).reshape(width, SPAN).T

    attn_part = jnp.dot(attention, out_weight, preferred_element_type=jnp.float32)
    (attn_out,) = reduce_scatter(
        grid,
        1,
        add_join,
        [attn_part.astype(jnp.bfloat16).reshape(wide, rows, -1)],
        [jnp.float32],
        4,
    )
    normed_mid = rms_scale(attn_out, mlp_gain)
    every_row = gather(grid, ("a", "b", "r", "c"), normed_mid, 5).reshape(reqs * SPAN, -1)
    both = jnp.einsum("td,cfd->ctf", every_row, gate_up, preferred_element_type=jnp.float32)
    hidden = (jax.nn.silu(both[0]) * both[1]).astype(jnp.bfloat16)
    mlp_part = jnp.dot(hidden, down_weight, preferred_element_type=jnp.float32)
    (hidden_out,) = reduce_scatter(
        grid,
        reqs,
        add_join,
        [mlp_part.astype(jnp.bfloat16).reshape(reqs * wide, rows, -1)],
        [jnp.bfloat16],
        6,
    )
    return (hidden_out, attention, new_keys, new_values)


def solution(mesh):
    grid = Grid(mesh.shape["req"], mesh.shape["wide"])
    return jax.shard_map(
        functools.partial(body, grid),
        mesh=mesh,
        in_specs=(
            P(("req", "wide"), None),
            P(),
            P(None, None, "wide"),
            P("wide", None),
            P(None, None, "wide"),
            P("wide", None),
            P(),
            P(None, ("req", "wide"), None),
            P(("req", "wide"), None),
            P("req", "wide", None),
            P("req", "wide", None),
            P("req"),
            P("req", "wide"),
            P("req"),
        ),
        out_specs=(P(("req", "wide"), None), P("req", "wide"), P("req", "wide"), P("req", "wide")),
        check_vma=False,
    )
```

time: 1050 us -> 183 us (0.17)
  waiting for transfers between devices: 581 us -> 0 us
  local copies, waits for them, and re-layouts: 210 us -> 5.55 us
  Pallas kernels: 0 us -> 156 us
  blocking collectives: 101 us -> 0 us
  other arithmetic: 103 us -> 3.46 us
  matrix products: 38 us -> 15.4 us
  between operations: 15.6 us -> 2.24 us
    all_gather x4 -> x0, waiting for transfers between devices: 381 us -> none  [the longest x1 247 us: joined_2(): pieces = jax.tree.map(lambda part: lax.all_gather(part, axis), value)]
    reduce_scatter x2 -> x0, waiting for transfers between devices: 200 us -> none  [the longest x1 139 us: body(): lax.psum_scatter(feed_forward(every_row, gate_up, down_weight), ('req', '...]
    pallas_call x0 -> x8, Pallas kernels: none -> 156 us  [the longest x3 67.7 us: reduce_scatter(): pl.pallas_call(functools.partial(reduce_kernel, grid, reqs, join, len(arr...]
    dynamic_slice x31 -> x0, local copies, waits for them, and re-layouts: 142 us -> none  [the longest x30 142 us: joined_2(): lax.scan(lambda so_far, slab: (join(so_far, slab), None), head, tail)]
    add x30 -> x1, other arithmetic: 90.7 us -> 0.01 us  [body(): totals = cache_sum * cache_factor + own_sum * own_factor]
    psum x1 -> x0, blocking collectives: 60.9 us -> none  [body(): lax.psum(united_rows[:, 3 * local_width:], 'wide').astype(jnp.bfloat16)]
    all_gather x2 -> x0, blocking collectives: 40.2 us -> none  [joined_2(): pieces = jax.tree.map(lambda part: lax.all_gather(part, axis), value)]
    slice x4 -> x0, local copies, waits for them, and re-layouts: 37.9 us -> none  [joined_2(): tail = jax.tree.map(lambda part: part[1:], pieces)]
  transfers between devices with their start and end apart: 6 -> 0, of which waited for: 6 -> 0; matrix products, arithmetic and copies ran while one was open for 0% -> 0% of each run, Pallas kernels for 0% -> 0%
where the time goes in v1:
time: 183 us
  Pallas kernels  156 us (85%)
  matrix products  15.4 us (8%)
  local copies, waits for them, and re-layouts  5.55 us (3%)
  other arithmetic  3.46 us (2%)
  between operations  2.24 us (1%)
    pallas_call x3, Pallas kernels, reduce_scatter(): pl.pallas_call(functools.partial(reduce_kernel, grid, reqs, join, len(arr...  67.7 us
    pallas_call x3, Pallas kernels, gather(): pl.pallas_call(functools.partial(gather_kernel, grid, order), out_shape=j...  63.7 us
    pallas_call x1, Pallas kernels, lowrank_sum(): pl.pallas_call(functools.partial(lowrank_kernel, grid), out_shape=jax.Sha...  15.5 us
    dot_general x1, matrix products, body(): jnp.dot(shard_rows, qkv_weight.reshape(D, 3 * width), preferred_element_t...  9.74 us
    pallas_call x1, Pallas kernels, cache_attention(): pl.pallas_call(functools.partial(cache_kernel, heads), grid=(HEADS // GRO...  9.33 us
    unnamed x23, local copies, waits for them, and re-layouts  4.68 us

profile of v1, /device:TPU:0, one launch (start us, length us, event | category | flops | bytes accessed | tf_op | source)
XLA Modules:
  0.0 182.9 jit_solution(2344947698457597802)
XLA Ops:
  0.6 0.0 copy-start
  0.7 0.9 convert_element_type.41
  1.5 1.2 fusion.16
  2.7 1.0 fusion.18.x_ref
  3.7 23.0 %gather0.1 = bf16[16,8,7168]{2,1,0:T(8,128)(2,1)S(1)} custom-call(bf16[8,7168]{1,0:T(8,128)(2,1)S(1)} %fusion.18.x_ref), custom_call_target="tpu_custom_call" | custom-call | tf_op jit(solution)/shard_map/gather0/pallas_call | solution.py:131
  26.8 1.2 copy-done.1
  28.0 1.2 convolution_bitcast_fusion.1.p_ref
  29.3 15.5 %lowrank_sum.1 = bf16[16,8,384]{2,1,0:T(8,128)(2,1)S(1)} custom-call(f32[16,8,384]{2,1,0:T(8,128)S(1)} %convolution_bitcast_fusion.1.p_ref), custom_call_target="tpu_custom_call" | custom-call | tf_op jit(solution)/shard_map/lowrank_sum/pallas_call | solution.py:180
  44.8 0.0 copy-start.5
  44.8 9.7 %fusion = f32[128,3,448]{0,2,1:T(8,128)S(1)} fusion(bf16[7168,3,448]{0,2,1:T(8,128)(2,1)} %param.16, bf16[16,8,7168]{2,1,0:T(8,128)(2,1)} %copy-done.1), kind=kOutput, calls=%fused_computation | convolution fusion | flops 2466250752 | bytes 21790720 | tf_op jit(solution)/shard_map/dot_general | solution.py:437
  54.5 0.3 fusion.9
  54.8 0.8 slice_bitcast_fusion.2
  56.2 0.1 fusion.28
  56.3 0.2 fusion.38
  56.6 20.0 %gather2.1 = bf16[16,2,224,128]{3,2,1,0:T(8,128)(2,1)S(1)} custom-call(bf16[2,224,128]{2,1,0:T(8,128)(2,1)S(1)} %bitcast.79), custom_call_target="tpu_custom_call" | custom-call | tf_op jit(solution)/shard_map/gather2/pallas_call | solution.py:131
  76.7 1.2 copy-done.2
  78.6 0.1 broadcast_in_dim.14.ok_ref
  78.7 1.5 copy-done.3
  80.2 9.3 %cache_attention.1 = (bf16[32,224,128]{2,1,0:T(8,128)(2,1)S(1)}, f32[16,8,128]{2,1,0:T(8,128)S(1)}) custom-call(bf16[32,224,128]{2,1,0:T(8,128)(2,1)S(1)} %bitcast.74, bf16[1,256,7168]{2,1,0:T(8,128)(2,1)} %k_ref.1, bf16[1,256,7168]{2,1,0:T(8,128)(2,1)} %v_ref.1, f32[256,128]{1,0:T(8,128)S(1)} %broadcast_in_dim.14.ok_ref), custom_call_target="tpu_custom_call" | custom-call | tf_op jit(solution)/shard_map/cache_attention/pallas_call | solution.py:388
  89.6 0.0 slice-start.1
  89.6 29.9 %reduce3.1 = (f32[2,224,128]{2,1,0:T(8,128)S(1)}, f32[8,128]{1,0:T(8,128)S(1)}) custom-call(bf16[1,4,2,2,2,224,128]{6,5,4,3,2,1,0:T(8,128)(2,1)S(1)} %bitcast.77, f32[1,4,2,2,8,128]{5,4,3,2,1,0:T(8,128)S(1)} %bitcast.80), custom_call_target="tpu_custom_call" | custom-call | tf_op jit(solution)/shard_map/reduce3/pallas_call | solution.py:351
  119.5 0.2 fusion.12
  119.7 0.0 copy-start.6
  119.7 0.7 convolution_convert_fusion.1
  120.4 16.3 %reduce4.1 = f32[8,3584]{1,0:T(8,128)S(1)} custom-call(bf16[1,4,2,2,8,3584]{5,4,3,2,1,0:T(8,128)(2,1)S(1)} %bitcast.76), custom_call_target="tpu_custom_call" | custom-call | tf_op jit(solution)/shard_map/reduce4/pallas_call | solution.py:351
  136.8 0.1 multiply_reduce_fusion
  136.9 0.1 multiply_convert_fusion.x_ref
  137.0 20.6 %gather5.1 = bf16[32,8,3584]{2,1,0:T(8,128)(2,1)S(1)} custom-call(bf16[8,3584]{1,0:T(8,128)(2,1)S(1)} %multiply_convert_fusion.x_ref), custom_call_target="tpu_custom_call" | custom-call | tf_op jit(solution)/shard_map/gather5/pallas_call | solution.py:131
  157.7 1.8 %fusion.5 = f32[2,256,448]{1,2,0:T(8,128)S(1)} fusion(bf16[2,448,3584]{2,1,0:T(8,128)(2,1)S(1)} %bitcast.86, bf16[32,8,3584]{2,1,0:T(8,128)(2,1)S(1)} %gather5.1), kind=kOutput, calls=%fused_computation.7 | convolution fusion | flops 1644167168 | bytes 9175040 | tf_op jit(solution)/shard_map/td,cfd->ctf/dot_general | solution.py:507
  159.5 1.2 convolution_convert_fusion
  160.7 21.5 %reduce6.1 = bf16[8,3584]{1,0:T(8,128)(2,1)S(1)} custom-call(bf16[2,4,2,2,8,3584]{5,4,3,2,1,0:T(8,128)(2,1)S(1)} %bitcast.75), custom_call_target="tpu_custom_call" | custom-call | tf_op jit(solution)/shard_map/reduce6/pallas_call | solution.py:351
  182.2 0.6 copy.25
  (25 shorter events, 0.2 us)
Async XLA Ops:
  0.6 158.9 %copy-start = (bf16[448,3584]{1,0:T(8,128)(2,1)S(1)}, bf16[448,3584]{1,0:T(8,128)(2,1)}, u32[]{:S(2)}) copy-start(bf16[448,3584]{1,0:T(8,128)(2,1)} %param.22) | copy-start | bytes 9633796
  26.7 1.3 copy-start.1
  44.8 9.8 %copy-start.5 = (bf16[3,128,448]{1,2,0:T(8,128)(2,1)S(1)}, bf16[3,128,448]{1,2,0:T(8,128)(2,1)}, u32[]{:S(2)}) copy-start(bf16[3,128,448]{1,2,0:T(8,128)(2,1)} %param.18) | copy-start | bytes 1032196
  54.5 24.0 %copy-start.8 = (s32[1,256]{1,0:T(1,128)S(1)}, s32[1,256]{1,0:T(1,128)}, u32[]{:S(2)}) copy-start(s32[1,256]{1,0:T(1,128)} %param.26) | copy-start | bytes 3076
  76.7 1.3 copy-start.2
  78.7 1.5 copy-start.3
  80.2 39.5 %copy-start.4 = (bf16[448,3584]{1,0:T(8,128)(2,1)S(1)}, bf16[448,3584]{1,0:T(8,128)(2,1)}, u32[]{:S(2)}) copy-start(bf16[448,3584]{1,0:T(8,128)(2,1)} %param.19) | copy-start | bytes 9633796
  80.2 77.4 %slice-start = ((s8[6422528]{0:T(1024)(128)(4,1)}), s8[2228224]{0:T(1024)(128)(4,1)S(1)}, s32[]{:S(2)}) async-start(s8[6422528]{0:T(1024)(128)(4,1)} %bitcast.85), calls=%async_computation | async-start | bytes 4456448
  89.6 68.1 %slice-start.1 = ((s8[6422528]{0:T(1024)(128)(4,1)}), s8[4194304]{0:T(1024)(128)(4,1)S(1)}, s32[]{:S(2)}) async-start(s8[6422528]{0:T(1024)(128)(4,1)} %bitcast.85), calls=%async_computation.1 | async-start | bytes 8388608
  119.5 17.4 %copy-start.7 = (bf16[3584]{0:T(1024)(128)(2,1)S(1)}, bf16[3584]{0:T(1024)(128)(2,1)}, u32[]{:S(2)}) copy-start(bf16[3584]{0:T(1024)(128)(2,1)} %param.20) | copy-start | bytes 21508
  119.7 37.9 %copy-start.6 = (bf16[2,224,128]{2,1,0:T(8,128)(2,1)}, bf16[2,224,128]{2,1,0:T(8,128)(2,1)S(1)}, u32[]{:S(2)}) copy-start(bf16[2,224,128]{2,1,0:T(8,128)(2,1)S(1)} %fusion.12) | copy-start | bytes 344068

commit v2 on v1

--- a/solution.py
+++ b/solution.py
@@ -1,4 +1,5 @@
 import functools
+import math
 
 import jax
 import jax.numpy as jnp
@@ -120,76 +121,162 @@
         copy.wait_send()
 
 
-def gather_kernel(grid, order, x_ref, o_ref, send, recv, local):
+def project_kernel(
+    grid,
+    window,
+    chunk,
+    x_ref,
+    w_hbm,
+    down_ref,
+    up_ref,
+    q_all,
+    q_ref,
+    nk_ref,
+    nv_ref,
+    w_ref,
+    xs,
+    xb,
+    acc,
+    p_ref,
+    r_ref,
+    t_ref,
+    low_ref,
+    q_own,
+    w_sems,
+    s1,
+    r1,
+    s2,
+    r2,
+    local,
+    sems,
+):
     me = grid.place()
-    grid.barrier(me, order)
-    spread(grid, me, order, x_ref, o_ref, send, recv, local)
-
-
-def gather(grid, order, x, collective_id):
-    slots = grid.wide * (grid.size["r"] if "r" in order else 1)
-    return pl.pallas_call(
-        functools.partial(gather_kernel, grid, order),
-        out_shape=jax.ShapeDtypeStruct((slots,) + x.shape, x.dtype),
-        in_specs=[pl.BlockSpec(memory_space=pltpu.VMEM)],
-        out_specs=pl.BlockSpec(memory_space=pltpu.VMEM),
-        scratch_shapes=[
-            pltpu.SemaphoreType.DMA((slots,)),
-            pltpu.SemaphoreType.DMA((slots,)),
-            pltpu.SemaphoreType.DMA,
-        ],
-        compiler_params=params(collective_id),
-        name="gather" + str(collective_id),
-    )(x)
-
-
-def lowrank_kernel(grid, p_ref, o_ref, r_ref, t_ref, sems):
-    me = lax.axis_index("wide")
-    req = lax.axis_index("req")
+    order = ("a", "b", "c")
     n = grid.wide
+    at = grid.on_wide(me)
+    rows = x_ref.shape[0]
+    width = q_ref.shape[0]
+    steps = 3 * width // chunk
+
+    def load(i):
+        part = pl.ds(i * chunk, chunk)
+        return pltpu.make_async_copy(w_hbm.at[part], w_ref.at[part], w_sems.at[i])
+
+    for i in range(steps):
+        load(i).start()
     barrier = pltpu.get_barrier_semaphore()
     for d in range(1, n):
-        pl.semaphore_signal(barrier, inc=1, device_id=(req, (me + d) % n), device_id_type=MESH)
+        pl.semaphore_signal(barrier, inc=1, device_id=(me["r"], (at + d) % n), device_id_type=MESH)
     pl.semaphore_wait(barrier, n - 1)
+    spread(grid, me, order, x_ref, xs, s1, r1, local.at[0])
+
+    def pack(i, carry):
+        cols = pl.ds(pl.multiple_of(i * 1024, 1024), 1024)
+        slabs = [xs[k, :, cols].astype(jnp.float32) for k in range(n)]
+        xb[:, cols] = jnp.concatenate(slabs, axis=0).astype(jnp.bfloat16)
+        return carry
+
+    lax.fori_loop(0, D // 1024, pack, 0)
+    xb[:, D:] = jnp.zeros((SPAN, xb.shape[1] - D), jnp.bfloat16)
+    base = pl.multiple_of(at * width // 128 * 128, 128)
+    partial = jnp.dot(xb[:, pl.ds(base, window)], down_ref[...], preferred_element_type=jnp.float32)
+    for k in range(n):
+        p_ref[k] = partial[k * rows : (k + 1) * rows]
     first = []
     for d in range(1, n):
-        to = (me + d) % n
-        copy = remote(p_ref.at[to], r_ref.at[d - 1], sems.at[0, d], sems.at[1, d], (req, to))
+        to = (at + d) % n
+        copy = remote(p_ref.at[to], r_ref.at[d - 1], sems.at[0, d], sems.at[1, d], (me["r"], to))
         copy.start()
         first.append(copy)
-    total = p_ref[me]
+
+    def multiply(i, carry):
+        load(i).wait()
+        part = pl.ds(pl.multiple_of(i * chunk, chunk), chunk)
+        acc[part, :] = lax.dot_general(
+            w_ref[part, :],
+            xb[:, :D],
+            (((1,), (1,)), ((), ())),
+            preferred_element_type=jnp.float32,
+        )
+        return carry
+
+    lax.fori_loop(0, steps // 2, multiply, 0)
+    total = p_ref[at]
     for d, copy in enumerate(first):
         copy.wait_recv()
         total = total + r_ref[d]
     t_ref[...] = total.astype(t_ref.dtype)
     second = []
     for d in range(1, n):
-        copy = remote(t_ref, o_ref.at[me], sems.at[2, d], sems.at[3, d], (req, (me + d) % n))
+        copy = remote(t_ref, low_ref.at[at], sems.at[2, d], sems.at[3, d], (me["r"], (at + d) % n))
         copy.start()
         second.append(copy)
-    o_ref[me] = t_ref[...]
+    low_ref[at] = t_ref[...]
+    lax.fori_loop(steps // 2, steps, multiply, 0)
     for d in range(1, n):
-        remote(t_ref, o_ref.at[(me + n - d) % n], sems.at[2, d], sems.at[3, d], (req, me)).wait_recv()
+        source = (at + n - d) % n
+        remote(
+            t_ref, low_ref.at[source], sems.at[2, d], sems.at[3, d], (me["r"], at)
+        ).wait_recv()
+    lowrank = jnp.concatenate([low_ref[k].astype(jnp.float32) for k in range(n)], axis=0).astype(
+        jnp.bfloat16
+    )
+    for c, out in enumerate((q_ref, nk_ref, nv_ref)):
+        adapted = lax.dot_general(
+            up_ref[c],
+            lowrank[:, c * RANK : (c + 1) * RANK],
+            (((1,), (1,)), ((), ())),
+            preferred_element_type=jnp.float32,
+        )
+        value = (acc[c * width : (c + 1) * width, :] + adapted).astype(jnp.bfloat16)
+        out[...] = value
+        if c == 0:
+            q_own[...] = value
+    spread(grid, me, order, q_own, q_all, s2, r2, local.at[1])
     for copy in first + second:
         copy.wait_send()
 
 
-def lowrank_sum(grid, partial, collective_id):
-    n, rows, width = partial.shape
+def project(grid, normed, qkv_weight, adapter_down, adapter_up, collective_id):
+    n = grid.wide
+    rows = normed.shape[0]
+    width = qkv_weight.shape[2]
+    window = -(-(width + 128 - math.gcd(width, 128)) // 128) * 128
+    shift = lax.axis_index("wide") * width % 128
+    down = lax.dynamic_update_slice(
+        jnp.zeros((window, 3 * RANK), jnp.bfloat16), adapter_down, (shift, 0)
+    )
+    weight = qkv_weight.transpose(1, 2, 0).reshape(3 * width, D)
+    chunk = 224 if width % 224 == 0 else width
     vmem = pl.BlockSpec(memory_space=pltpu.VMEM)
+    turned = jax.ShapeDtypeStruct((width, SPAN), jnp.bfloat16)
+    dma = pltpu.SemaphoreType.DMA
     return pl.pallas_call(
-        functools.partial(lowrank_kernel, grid),
-        out_shape=jax.ShapeDtypeStruct(partial.shape, jnp.bfloat16),
-        in_specs=[vmem],
-        out_specs=vmem,
+        functools.partial(project_kernel, grid, window, chunk),
+        out_shape=[jax.ShapeDtypeStruct((n, width, SPAN), jnp.bfloat16), turned, turned, turned],
+        in_specs=[vmem, pl.BlockSpec(memory_space=pl.ANY), vmem, vmem],
+        out_specs=[vmem] * 4,
         scratch_shapes=[
-            pltpu.VMEM((n - 1, rows, width), jnp.float32),
-            pltpu.VMEM((rows, width), jnp.bfloat16),
-            pltpu.SemaphoreType.DMA((4, n)),
+            pltpu.VMEM((3 * width, D), jnp.bfloat16),
+            pltpu.VMEM((n, rows, D), jnp.bfloat16),
+            pltpu.VMEM((SPAN, D + 256), jnp.bfloat16),
+            pltpu.VMEM((3 * width, SPAN), jnp.float32),
+            pltpu.VMEM((n, rows, 3 * RANK), jnp.float32),
+            pltpu.VMEM((n - 1, rows, 3 * RANK), jnp.float32),
+            pltpu.VMEM((rows, 3 * RANK), jnp.bfloat16),
+            pltpu.VMEM((n, rows, 3 * RANK), jnp.bfloat16),
+            pltpu.VMEM((width, SPAN), jnp.bfloat16),
+            dma((3 * width // chunk,)),
+            dma((n,)),
+            dma((n,)),
+            dma((n,)),
+            dma((n,)),
+            dma((2,)),
+            dma((4, n)),
         ],
         compiler_params=params(collective_id),
-        name="lowrank_sum",
-    )(partial)
+        name="project",
+    )(normed, weight, down, adapter_up.transpose(0, 2, 1))
 
 
 def add_join(first, second):
@@ -359,6 +446,41 @@
     )(*[x.reshape((reqs, A, B, 2) + x.shape[1:]) for x in arrays])
 
 
+def middle_kernel(grid, p_ref, gain_ref, o_ref, mid_ref, *rest):
+    scratch, sems, send, recv, local = rest[:-4], rest[-4], rest[-3], rest[-2], rest[-1]
+    sc = {name: [scratch[k]] for k, name in enumerate(SCRATCH)}
+    me = grid.place()
+    grid.barrier(me, ("r", "a", "b", "c"))
+    (total,), sends = combine_down(grid, me, 1, add_join, [p_ref], sc, sems)
+    meansq = jnp.mean(total * total, axis=-1, keepdims=True)
+    scaled = total * lax.rsqrt(meansq + EPSILON) * gain_ref[...].astype(jnp.float32)
+    mid_ref[...] = scaled.astype(mid_ref.dtype)
+    spread(grid, me, ("a", "b", "r", "c"), mid_ref, o_ref, send, recv, local)
+    for copy in sends:
+        copy.wait_send()
+
+
+def middle(grid, part, gain, collective_id):
+    slots = grid.size["r"] * grid.wide
+    slab = part.shape[1:]
+    vmem = pl.BlockSpec(memory_space=pltpu.VMEM)
+    return pl.pallas_call(
+        functools.partial(middle_kernel, grid),
+        out_shape=jax.ShapeDtypeStruct((slots,) + slab, jnp.bfloat16),
+        in_specs=[vmem, vmem],
+        out_specs=vmem,
+        scratch_shapes=[pltpu.VMEM(slab, jnp.bfloat16)]
+        + reduce_scratch(grid, 1, [(slab, jnp.bfloat16)])
+        + [
+            pltpu.SemaphoreType.DMA((slots,)),
+            pltpu.SemaphoreType.DMA((slots,)),
+            pltpu.SemaphoreType.DMA,
+        ],
+        compiler_params=params(collective_id),
+        name="middle",
+    )(part.reshape((1, grid.size["a"], grid.size["b"], 2) + slab), gain.reshape(1, -1))
+
+
 def cache_kernel(heads, q_ref, k_ref, v_ref, ok_ref, num_ref, st_ref):
     ok = ok_ref[...] > 0.0
     st_ref[...] = jnp.zeros_like(st_ref)
@@ -430,23 +552,13 @@
     heads = width // HD
     wide_index = lax.axis_index("wide")
     normed = rms_scale(tokens, attn_gain)
-    shard_rows = gather(grid, ("a", "b", "c"), normed, 0).reshape(SPAN, D)
-    sliced = lax.dynamic_slice_in_dim(shard_rows, wide_index * width, width, 1)
-    partial_low = jnp.dot(sliced, adapter_down, preferred_element_type=jnp.float32)
-    lowrank = lowrank_sum(grid, partial_low.reshape(wide, rows, 3 * RANK), 1)
-    base = jnp.dot(shard_rows, qkv_weight.reshape(D, 3 * width), preferred_element_type=jnp.float32)
-    adapted = jnp.einsum(
-        "tcr,crd->tcd",
-        lowrank.reshape(SPAN, 3, RANK),
-        adapter_up,
-        preferred_element_type=jnp.float32,
-    )
-    projected = (base.reshape(SPAN, 3, width) + adapted).astype(jnp.bfloat16)
-    query_own = projected[:, 0]
-    new_keys = projected[:, 1]
-    new_values = projected[:, 2]
-    query_turned = query_own.T.reshape(heads, HD, SPAN)
-    query_all = gather(grid, ("a", "b", "c"), query_turned, 2).reshape(HEADS, HD, SPAN)
+    query_all, query_turned, keys_turned, values_turned = project(
+        grid, normed, qkv_weight, adapter_down, adapter_up, 0
+    )
+    new_keys = keys_turned.T
+    new_values = values_turned.T
+    query_all = query_all.reshape(HEADS, HD, SPAN)
+    query_turned = query_turned.reshape(heads, HD, SPAN)
 
     block_len = key_cache.shape[1]
     positions = wide_index * block_len + jnp.arange(block_len)
@@ -494,16 +606,9 @@
     attention = (mixed / totals[:, None]).astype(jnp.bfloat16).reshape(width, SPAN).T
 
     attn_part = jnp.dot(attention, out_weight, preferred_element_type=jnp.float32)
-    (attn_out,) = reduce_scatter(
-        grid,
-        1,
-        add_join,
-        [attn_part.astype(jnp.bfloat16).reshape(wide, rows, -1)],
-        [jnp.float32],
-        4,
-    )
-    normed_mid = rms_scale(attn_out, mlp_gain)
-    every_row = gather(grid, ("a", "b", "r", "c"), normed_mid, 5).reshape(reqs * SPAN, -1)
+    every_row = middle(
+        grid, attn_part.astype(jnp.bfloat16).reshape(wide, rows, -1), mlp_gain, 4
+    ).reshape(reqs * SPAN, -1)
     both = jnp.einsum("td,cfd->ctf", every_row, gate_up, preferred_element_type=jnp.float32)
     hidden = (jax.nn.silu(both[0]) * both[1]).astype(jnp.bfloat16)
     mlp_part = jnp.dot(hidden, down_weight, preferred_element_type=jnp.float32)

time: 183 us -> 171 us (0.934)
  matrix products: 15.4 us -> 4.13 us
  Pallas kernels: 156 us -> 153 us
  local copies, waits for them, and re-layouts: 5.55 us -> 7.5 us
    pallas_call x3 -> x2, Pallas kernels: 67.7 us -> 54.6 us  [reduce_scatter(): pl.pallas_call(functools.partial(reduce_kernel, grid, reqs, join, len(arr...]
    dot_general x3 -> x0, matrix products: 11.2 us -> none  [the longest x1 9.74 us: body(): jnp.dot(shard_rows, qkv_weight.reshape(D, 3 * width), preferred_element_t...]
    pallas_call x4 -> x2, Pallas kernels: 79.2 us -> 89.5 us  [the longest x1 55.8 us: project(): pl.pallas_call(functools.partial(project_kernel, grid, window, chunk), ou...]
    unnamed x23 -> x25, local copies, waits for them, and re-layouts: 4.68 us -> 6.32 us
where the time goes in v2:
time: 171 us; the launch traced here: 170 us
  Pallas kernels  153 us (89%)
  local copies, waits for them, and re-layouts  7.5 us (4%)
  matrix products  4.13 us (2%)
  other arithmetic  3.23 us (2%)
  between operations  2.2 us (1%)
    pallas_call x1, Pallas kernels, project(): pl.pallas_call(functools.partial(project_kernel, grid, window, chunk), ou...  55.8 us
    pallas_call x2, Pallas kernels, reduce_scatter(): pl.pallas_call(functools.partial(reduce_kernel, grid, reqs, join, len(arr...  54.6 us
    pallas_call x1, Pallas kernels, middle(): pl.pallas_call(functools.partial(middle_kernel, grid), out_shape=jax.Shap...  33.6 us
    pallas_call x1, Pallas kernels, cache_attention(): pl.pallas_call(functools.partial(cache_kernel, heads), grid=(HEADS // GRO...  9.21 us
    unnamed x25, local copies, waits for them, and re-layouts  6.32 us

profile of v2, /device:TPU:0, one launch (start us, length us, event | category | flops | bytes accessed | tf_op | source)
XLA Modules:
  0.0 170.3 jit_solution(13255223208932901049)
XLA Ops:
  0.6 0.0 copy-start
  0.6 0.9 convert_element_type.32
  1.5 1.2 fusion.11
  2.7 1.0 fusion.13.x_ref
  3.8 1.0 constant_dynamic-update-slice_fusion.down_ref
  4.8 0.0 copy-start.3
  4.8 1.0 copy-done.3
  5.8 55.8 %project.1 = (bf16[16,448,128]{2,1,0:T(8,128)(2,1)S(1)}, bf16[448,128]{1,0:T(8,128)(2,1)S(1)}, bf16[448,128]{1,0:T(8,128)(2,1)S(1)}, bf16[448,128]{1,0:T(8,128)(2,1)S(1)}) custom-call(bf16[8,7168]{1,0:T(8,128)(2,1)S(1)} %fusion.13.x_ref, bf16[1344,7168]{1,0:T(8,128)(2,1)} %bitcast.62, bf16[512,384]{1,0:T(8,128)(2,1)S(1)} %constant_dynamic-update-slice_fusion.down_ref, ...), custom_call_target="tpu_custom_call" | custom-call | tf_op jit(solution)/shard_map/project/pallas_call | solution.py:254
  61.6 1.2 copy-done.1
  62.9 0.6 copy-done.4
  64.2 0.1 broadcast_in_dim.30.ok_ref
  64.3 1.5 copy-done.2
  65.8 9.2 %cache_attention.1 = (bf16[32,224,128]{2,1,0:T(8,128)(2,1)S(1)}, f32[16,8,128]{2,1,0:T(8,128)S(1)}) custom-call(bf16[32,224,128]{2,1,0:T(8,128)(2,1)S(1)} %bitcast.54, bf16[1,256,7168]{2,1,0:T(8,128)(2,1)} %k_ref.1, bf16[1,256,7168]{2,1,0:T(8,128)(2,1)} %v_ref.1, f32[256,128]{1,0:T(8,128)S(1)} %broadcast_in_dim.30.ok_ref), custom_call_target="tpu_custom_call" | custom-call | tf_op jit(solution)/shard_map/cache_attention/pallas_call | solution.py:510
  75.0 0.0 copy-start.6
  75.1 30.4 %reduce3.1 = (f32[2,224,128]{2,1,0:T(8,128)S(1)}, f32[8,128]{1,0:T(8,128)S(1)}) custom-call(bf16[1,4,2,2,2,224,128]{6,5,4,3,2,1,0:T(8,128)(2,1)S(1)} %bitcast.53, f32[1,4,2,2,8,128]{5,4,3,2,1,0:T(8,128)S(1)} %bitcast.61), custom_call_target="tpu_custom_call" | custom-call | tf_op jit(solution)/shard_map/reduce3/pallas_call | solution.py:438
  105.5 0.0 copy-start.8
  106.1 0.1 fusion.21
  106.2 0.2 fusion.30
  106.6 0.2 fusion.7
  106.7 0.0 copy-start.7
  106.8 0.0 copy-start.9
  106.8 0.7 convolution_convert_fusion.1
  107.5 0.0 copy-done.8
  107.5 33.6 %middle.1 = bf16[32,8,3584]{2,1,0:T(8,128)(2,1)S(1)} custom-call(bf16[1,4,2,2,8,3584]{5,4,3,2,1,0:T(8,128)(2,1)S(1)} %bitcast.52, bf16[1,3584]{1,0:T(2,128)(2,1)S(1)} %reshape.74.gain_ref), custom_call_target="tpu_custom_call" | custom-call | tf_op jit(solution)/shard_map/middle/pallas_call | solution.py:467
  141.1 0.0 copy-done.7
  141.1 0.0 copy-done.9
  141.1 1.9 %fusion.2 = f32[2,256,448]{1,2,0:T(8,128)S(1)} fusion(bf16[2,448,3584]{2,1,0:T(8,128)(2,1)S(1)} %copy-done.9, bf16[32,8,3584]{2,1,0:T(8,128)(2,1)S(1)} %middle.1), kind=kOutput, calls=%fused_computation.4 | convolution fusion | flops 1644167168 | bytes 9175040 | tf_op jit(solution)/shard_map/td,cfd->ctf/dot_general | solution.py:612
  143.0 1.2 convolution_convert_fusion
  144.2 24.2 %reduce6.1 = bf16[8,3584]{1,0:T(8,128)(2,1)S(1)} custom-call(bf16[2,4,2,2,8,3584]{5,4,3,2,1,0:T(8,128)(2,1)S(1)} %bitcast.51), custom_call_target="tpu_custom_call" | custom-call | tf_op jit(solution)/shard_map/reduce6/pallas_call | solution.py:438
  168.4 0.6 copy.24
  169.0 0.6 copy.25
  169.7 0.6 copy.26
  (17 shorter events, 0.2 us)
Async XLA Ops:
  0.6 142.4 %copy-start = (bf16[448,3584]{1,0:T(8,128)(2,1)S(1)}, bf16[448,3584]{1,0:T(8,128)(2,1)}, u32[]{:S(2)}) copy-start(bf16[448,3584]{1,0:T(8,128)(2,1)} %param.22) | copy-start | bytes 9633796
  4.8 1.0 copy-start.3
  5.8 57.7 %copy-start.10 = (s32[1,256]{1,0:T(1,128)S(1)}, s32[1,256]{1,0:T(1,128)}, u32[]{:S(2)}) copy-start(s32[1,256]{1,0:T(1,128)} %param.26) | copy-start | bytes 3076
  61.6 1.3 copy-start.1
  62.9 0.6 copy-start.4
  64.3 1.5 copy-start.2
  65.8 40.4 %copy-start.5 = (bf16[448,128]{1,0:T(8,128)(2,1)S(1)}, bf16[448,128]{1,0:T(8,128)(2,1)}, u32[]{:S(2)}) copy-start(bf16[448,128]{1,0:T(8,128)(2,1)} %copy-done.4) | copy-start | bytes 344068
  75.0 31.7 %copy-start.6 = (bf16[448,3584]{1,0:T(8,128)(2,1)S(1)}, bf16[448,3584]{1,0:T(8,128)(2,1)}, u32[]{:S(2)}) copy-start(bf16[448,3584]{1,0:T(8,128)(2,1)} %param.19) | copy-start | bytes 9633796
  105.5 2.0 %copy-start.8 = (bf16[3584]{0:T(1024)(128)(2,1)S(1)}, bf16[3584]{0:T(1024)(128)(2,1)}, u32[]{:S(2)}) copy-start(bf16[3584]{0:T(1024)(128)(2,1)} %param.20) | copy-start | bytes 21508
  106.7 34.4 %copy-start.7 = (bf16[2,224,128]{2,1,0:T(8,128)(2,1)}, bf16[2,224,128]{2,1,0:T(8,128)(2,1)S(1)}, u32[]{:S(2)}) copy-start(bf16[2,224,128]{2,1,0:T(8,128)(2,1)S(1)} %fusion.7) | copy-start | bytes 344068
  106.8 34.4 %copy-start.9 = (bf16[2,448,3584]{2,1,0:T(8,128)(2,1)S(1)}, bf16[2,448,3584]{2,1,0:T(8,128)(2,1)}, u32[]{:S(2)}) copy-start(bf16[2,448,3584]{2,1,0:T(8,128)(2,1)} %param.21) | copy-start | bytes 19267588

commit v3 on v2

--- a/solution.py
+++ b/solution.py
@@ -302,148 +302,289 @@
     return [num, jnp.concatenate([highest, sum1 * f1 + sum2 * f2], axis=-2)]
 
 
-def combine_down(grid, me, reqs, join, ps, sc, sems):
+def loop(count, step):
+    if count == 1:
+        step(0)
+    else:
+        lax.fori_loop(0, count, lambda i, carry: (step(i), carry)[1], 0)
+
+
+def combine_down(grid, me, reqs, join, ps, sc, sems, produce=None):
     R, A, B = reqs, grid.size["a"], grid.size["b"]
     r, a, b, c = (me["r"] if R > 1 else 0), me["a"], me["b"], me["c"]
-    parts = range(len(ps))
-    sends = []
-    count = [0]
-
-    def push(pairs, device):
-        out = []
-        for i, (src, dst) in enumerate(pairs):
-            k = count[0]
-            count[0] += 1
-            copy = remote(src, dst, sems.at[0, k], sems.at[1, k], device)
+    n = len(ps)
+    parts = range(n)
+    base_r = R * B * A * n
+    base_b = base_r + (R - 1) * B * A * n
+    base_a = base_b + (B - 1) * A * n
+    db_order = list(range(1, B)) + [0]
+    dr_order = list(range(1, R)) + [0]
+
+    def where(dr, db, i):
+        rr = (r + dr) % R if dr else r
+        bb = (b + db) % B if db else b
+        return rr, (a + i + 1) % A, bb
+
+    def copies(base, pairs, device):
+        return [
+            remote(src, dst, sems.at[0, base + k], sems.at[1, base + k], device)
+            for k, (src, dst) in enumerate(pairs)
+        ]
+
+    def core(dr, db, i):
+        rr, aa, bb = where(dr, db, i)
+        return copies(
+            ((dr * B + db) * A + i) * n,
+            [(ps[k].at[rr, aa, bb, 1 - c], sc["r1"][k].at[dr, db, i]) for k in parts],
+            grid.device(grid.moved(me, c=1)),
+        )
+
+    def along_r(dr, db, i):
+        return copies(
+            base_r + (((dr - 1) * B + db) * A + i) * n,
+            [(sc["t1"][k].at[dr - 1, db, i], sc["r2"][k].at[dr - 1, db, i]) for k in parts],
+            grid.device(grid.moved(me, r=dr)),
+        )
+
+    def along_b(db, i):
+        return copies(
+            base_b + ((db - 1) * A + i) * n,
+            [(sc["t2"][k].at[db - 1, i], sc["r3"][k].at[db - 1, i]) for k in parts],
+            grid.device(grid.moved(me, b=db)),
+        )
+
+    def along_a(da):
+        return copies(
+            base_a + (da - 1) * n,
+            [(sc["t3"][k].at[da - 1], sc["r4"][k].at[da - 1]) for k in parts],
+            grid.device(dict(me, a=(a + da) % A)),
+        )
+
+    def start(made):
+        for copy in made:
             copy.start()
-            out.append(copy)
-        sends.extend(out)
-        return out
-
-    def arrived(copies):
-        for copy in copies:
+
+    def arrived(made):
+        for copy in made:
             copy.wait_recv()
 
     def wide_values(refs):
         return [ref[...].astype(jnp.float32) for ref in refs]
 
-    others = list(range(1, B)) + [0]
-    core = {}
-    peer = grid.device(grid.moved(me, c=1))
-    for dr in list(range(1, R)) + [0]:
-        rr = (r + dr) % R if dr else r
-        for db in others:
-            bb = (b + db) % B if db else b
-            core[dr, db] = push(
-                [(ps[i].at[rr, :, bb, 1 - c], sc["r1"][i].at[rr, bb]) for i in parts], peer
-            )
-    along_r = {}
-    for dr in range(1, R):
-        rr = (r + dr) % R
-        for db in others:
-            bb = (b + db) % B if db else b
-            arrived(core[dr, db])
-            both = join(
-                wide_values([ps[i].at[rr, :, bb, c] for i in parts]),
-                wide_values([sc["r1"][i].at[rr, bb] for i in parts]),
-            )
-            for i in parts:
-                sc["t1"][i][rr, bb] = both[i].astype(sc["t1"][i].dtype)
-            along_r[dr, db] = push(
-                [(sc["t1"][i].at[rr, bb], sc["r2"][i].at[dr - 1, bb]) for i in parts],
-                grid.device(grid.moved(me, r=dr)),
-            )
-    along_b = {}
-    for db in others:
-        bb = (b + db) % B if db else b
-        arrived(core[0, db])
+    def at_chip(dr, db, i):
+        rr, aa, bb = where(dr, db, i)
+        arrived(core(dr, db, i))
         both = join(
-            wide_values([ps[i].at[r, :, bb, c] for i in parts]),
-            wide_values([sc["r1"][i].at[r, bb] for i in parts]),
-        )
+            wide_values([ps[k].at[rr, aa, bb, c] for k in parts]),
+            wide_values([sc["r1"][k].at[dr, db, i] for k in parts]),
+        )
+        if dr == 0:
+            for step in range(1, R):
+                arrived(along_r(step, db, i))
+                both = join(both, wide_values([sc["r2"][k].at[step - 1, db, i] for k in parts]))
+        return both
+
+    def keep(name, at, values):
+        for k in parts:
+            sc[name][k][at] = values[k].astype(sc[name][k].dtype)
+
+    def to_r(dr, db, i):
+        keep("t1", (dr - 1, db, i), at_chip(dr, db, i))
+        start(along_r(dr, db, i))
+
+    def to_b(db, i):
+        keep("t2", (db - 1, i), at_chip(0, db, i))
+        start(along_b(db, i))
+
+    def on_b(i):
+        both = at_chip(0, 0, i)
+        for db in range(1, B):
+            arrived(along_b(db, i))
+            both = join(both, wide_values([sc["r3"][k].at[db - 1, i] for k in parts]))
+        return both
+
+    def to_a(i):
+        keep("t3", (i,), on_b(i))
+        start(along_a(i + 1))
+
+    if produce is None:
+        for dr in dr_order:
+            for db in db_order:
+                loop(A, lambda i: start(core(dr, db, i)))
         for dr in range(1, R):
-            arrived(along_r[dr, db])
-            both = join(both, wide_values([sc["r2"][i].at[dr - 1, bb] for i in parts]))
-        if db:
-            for i in parts:
-                sc["t2"][i][bb] = both[i].astype(sc["t2"][i].dtype)
-            along_b[db] = push(
-                [(sc["t2"][i].at[bb], sc["r3"][i].at[db - 1]) for i in parts],
-                grid.device(grid.moved(me, b=db)),
-            )
-    for db in range(1, B):
-        arrived(along_b[db])
-        both = join(both, wide_values([sc["r3"][i].at[db - 1] for i in parts]))
-    for i in parts:
-        sc["own"][i][...] = both[i]
-        sc["t3"][i][...] = both[i].astype(sc["t3"][i].dtype)
-    along_a = []
+            for db in db_order:
+                loop(A, lambda i: to_r(dr, db, i))
+        for db in range(1, B):
+            loop(A, lambda i: to_b(db, i))
+    else:
+        before = None
+        for db in db_order:
+
+            def step(i):
+                produce(where(0, db, i))
+                start(core(0, db, i))
+                if before:
+                    pl.when(i == 0)(lambda: to_b(before, A - 1))
+                if db:
+                    pl.when(i > 0)(lambda: to_b(db, i - 1))
+
+            lax.fori_loop(0, A, lambda i, carry: (step(i), carry)[1], 0)
+            before = db
+    if A > 1:
+        loop(A - 1, to_a)
+    total = on_b(A - 1)
     for da in range(1, A):
-        aa = (a + da) % A
-        along_a.append(
-            push(
-                [(sc["t3"][i].at[aa], sc["r4"][i].at[da - 1]) for i in parts],
-                grid.device(grid.moved(me, a=da)),
-            )
-        )
-    total = [sc["own"][i][a] for i in parts]
-    for da in range(1, A):
-        arrived(along_a[da - 1])
-        total = join(total, wide_values([sc["r4"][i].at[da - 1] for i in parts]))
-    return total, sends
-
-
-SCRATCH = ("r1", "t1", "r2", "t2", "r3", "own", "t3", "r4")
+        arrived(along_a(da))
+        total = join(total, wide_values([sc["r4"][k].at[da - 1] for k in parts]))
+
+    def finish():
+        def sent(made):
+            for copy in made:
+                copy.wait_send()
+
+        for dr in range(R):
+            for db in range(B):
+                loop(A, lambda i: sent(core(dr, db, i)))
+                if dr:
+                    loop(A, lambda i: sent(along_r(dr, db, i)))
+        for db in range(1, B):
+            loop(A, lambda i: sent(along_b(db, i)))
+        for da in range(1, A):
+            sent(along_a(da))
+
+    return total, finish
+
+
+SCRATCH = ("r1", "t1", "r2", "t2", "r3", "t3", "r4")
 
 
 def reduce_scratch(grid, reqs, slabs):
     R, A, B = reqs, grid.size["a"], grid.size["b"]
     lead = dict(
         r1=(R, B, A),
-        t1=(R if R > 1 else 1, B if R > 1 else 1, A if R > 1 else 1),
+        t1=(R - 1, B, A) if R > 1 else (1, 1, 1),
         r2=(R - 1, B, A) if R > 1 else (1, 1, 1),
-        t2=(B, A),
+        t2=(max(B - 1, 1), A),
         r3=(max(B - 1, 1), A),
-        own=(A,),
-        t3=(A,),
+        t3=(max(A - 1, 1),),
         r4=(max(A - 1, 1),),
     )
-    shapes = []
-    for name in SCRATCH:
-        for shape, dtype in slabs:
-            shapes.append(
-                pltpu.VMEM(lead[name] + tuple(shape), jnp.float32 if name == "own" else dtype)
-            )
-    copies = (R * B + (R - 1) * B + (B - 1) + (A - 1)) * len(slabs)
-    shapes.append(pltpu.SemaphoreType.DMA((2, copies)))
+    shapes = [
+        pltpu.VMEM(lead[name] + tuple(shape), dtype) for name in SCRATCH for shape, dtype in slabs
+    ]
+    count = (R * B * A + (R - 1) * B * A + (B - 1) * A + (A - 1)) * len(slabs)
+    shapes.append(pltpu.SemaphoreType.DMA((2, count)))
     return shapes
 
 
-def reduce_kernel(grid, reqs, join, parts, *refs):
-    ps, outs, rest, sems = refs[:parts], refs[parts : 2 * parts], refs[2 * parts : -1], refs[-1]
-    sc = {name: rest[k * parts : (k + 1) * parts] for k, name in enumerate(SCRATCH)}
+def reduce_kernel(grid, reqs, p_ref, o_ref, *rest):
+    sems = rest[-1]
+    sc = {name: [rest[k]] for k, name in enumerate(SCRATCH)}
     me = grid.place()
-    grid.barrier(me, ("r", "a", "b", "c") if reqs > 1 else ("a", "b", "c"))
-    total, sends = combine_down(grid, me, reqs, join, ps, sc, sems)
-    for out, value in zip(outs, total):
-        out[...] = value.astype(out.dtype)
-    for copy in sends:
-        copy.wait_send()
-
-
-def reduce_scatter(grid, reqs, join, arrays, out_dtypes, collective_id):
-    A, B = grid.size["a"], grid.size["b"]
-    slabs = [(x.shape[1:], x.dtype) for x in arrays]
+    grid.barrier(me, ("r", "a", "b", "c"))
+    (total,), finish = combine_down(grid, me, reqs, add_join, [p_ref], sc, sems)
+    o_ref[...] = total.astype(o_ref.dtype)
+    finish()
+
+
+def reduce_scatter(grid, reqs, x, out_dtype, collective_id):
+    slab = x.shape[1:]
     vmem = pl.BlockSpec(memory_space=pltpu.VMEM)
     return pl.pallas_call(
-        functools.partial(reduce_kernel, grid, reqs, join, len(arrays)),
-        out_shape=[jax.ShapeDtypeStruct(s, t) for (s, _), t in zip(slabs, out_dtypes)],
-        in_specs=[vmem] * len(arrays),
-        out_specs=[vmem] * len(arrays),
-        scratch_shapes=reduce_scratch(grid, reqs, slabs),
+        functools.partial(reduce_kernel, grid, reqs),
+        out_shape=jax.ShapeDtypeStruct(slab, out_dtype),
+        in_specs=[vmem],
+        out_specs=vmem,
+        scratch_shapes=reduce_scratch(grid, reqs, [(slab, x.dtype)]),
         compiler_params=params(collective_id),
         name="reduce" + str(collective_id),
-    )(*[x.reshape((reqs, A, B, 2) + x.shape[1:]) for x in arrays])
+    )(x.reshape((reqs, grid.size["a"], grid.size["b"], 2) + slab))
+
+
+def cache_kernel(
+    grid, heads, q_ref, k_hbm, v_hbm, ok_ref, num_out, st_out, k_ref, v_ref, num, st, loads, *rest
+):
+    sems = rest[-1]
+    sc = {name: rest[2 * k : 2 * k + 2] for k, name in enumerate(SCRATCH)}
+    me = grid.place()
+    B = grid.size["b"]
+    groups = HEADS // GROUP
+    slabs = GROUP // heads
+
+    def load(g):
+        cols = pl.ds(pl.multiple_of(g * GROUP * HD, GROUP * HD), GROUP * HD)
+        return [
+            pltpu.make_async_copy(hbm.at[0, :, cols], ref.at[g], loads.at[k, g])
+            for k, (hbm, ref) in enumerate(((k_hbm, k_ref), (v_hbm, v_ref)))
+        ]
+
+    def group(g):
+        for copy in load(g):
+            copy.wait()
+        ok = ok_ref[...] > 0.0
+        for j in range(slabs):
+            slab = g * slabs + j
+            at = (0, slab // (2 * B), (slab // 2) % B, slab % 2)
+            tops, sums = [], []
+            for h in range(heads):
+                lanes = slice((j * heads + h) * HD, (j * heads + h + 1) * HD)
+                scores = jnp.dot(
+                    k_ref[g, :, lanes], q_ref[slab, h], preferred_element_type=jnp.float32
+                ) * HD ** (-0.5)
+                scores = jnp.where(ok, scores, NEG_LARGE)
+                top = jnp.max(scores, axis=0, keepdims=True)
+                weights = jnp.where(ok, jnp.exp(scores - top), 0.0)
+                num[at + (h,)] = lax.dot_general(
+                    v_ref[g, :, lanes],
+                    weights.astype(jnp.bfloat16),
+                    (((0,), (0,)), ((), ())),
+                    preferred_element_type=jnp.float32,
+                ).astype(jnp.bfloat16)
+                tops.append(top)
+                sums.append(jnp.sum(weights, axis=0, keepdims=True))
+            blank = [jnp.zeros((GROUP - heads, SPAN), jnp.float32)]
+            st[at] = jnp.concatenate(tops + blank + sums + blank, axis=0)
+
+    loop(groups, lambda g: [copy.start() for copy in load(g)] and None)
+    grid.barrier(me, ("a", "b", "c"))
+    if slabs == 2:
+        produce = lambda place: group(place[1] * B + place[2])
+    else:
+        loop(groups, group)
+        produce = None
+    total, finish = combine_down(grid, me, 1, softmax_join, [num, st], sc, sems, produce)
+    num_out[...] = total[0]
+    st_out[...] = total[1]
+    finish()
+
+
+def cache_attention(grid, heads, query, keys, values, usable, collective_id):
+    block = keys.shape[1]
+    groups = HEADS // GROUP
+    lead = (1, grid.size["a"], grid.size["b"], 2)
+    num = ((heads, HD, SPAN), jnp.bfloat16)
+    stats = ((2 * GROUP, SPAN), jnp.float32)
+    vmem = pl.BlockSpec(memory_space=pltpu.VMEM)
+    hbm = pl.BlockSpec(memory_space=pl.ANY)
+    return pl.pallas_call(
+        functools.partial(cache_kernel, grid, heads),
+        in_specs=[vmem, hbm, hbm, vmem],
+        out_specs=[vmem, vmem],
+        out_shape=[
+            jax.ShapeDtypeStruct(num[0], jnp.float32),
+            jax.ShapeDtypeStruct(stats[0], jnp.float32),
+        ],
+        scratch_shapes=[
+            pltpu.VMEM((groups, block, GROUP * HD), jnp.bfloat16),
+            pltpu.VMEM((groups, block, GROUP * HD), jnp.bfloat16),
+            pltpu.VMEM(lead + num[0], num[1]),
+            pltpu.VMEM(lead + stats[0], stats[1]),
+            pltpu.SemaphoreType.DMA((2, groups)),
+        ]
+        + reduce_scratch(grid, 1, [num, stats]),
+        compiler_params=params(collective_id),
+        name="cache_attention",
+    )(query, keys, values, usable)
 
 
 def middle_kernel(grid, p_ref, gain_ref, o_ref, mid_ref, *rest):
@@ -451,13 +592,12 @@
     sc = {name: [scratch[k]] for k, name in enumerate(SCRATCH)}
     me = grid.place()
     grid.barrier(me, ("r", "a", "b", "c"))
-    (total,), sends = combine_down(grid, me, 1, add_join, [p_ref], sc, sems)
+    (total,), finish = combine_down(grid, me, 1, add_join, [p_ref], sc, sems)
     meansq = jnp.mean(total * total, axis=-1, keepdims=True)
     scaled = total * lax.rsqrt(meansq + EPSILON) * gain_ref[...].astype(jnp.float32)
     mid_ref[...] = scaled.astype(mid_ref.dtype)
     spread(grid, me, ("a", "b", "r", "c"), mid_ref, o_ref, send, recv, local)
-    for copy in sends:
-        copy.wait_send()
+    finish()
 
 
 def middle(grid, part, gain, collective_id):
@@ -479,54 +619,6 @@
         compiler_params=params(collective_id),
         name="middle",
     )(part.reshape((1, grid.size["a"], grid.size["b"], 2) + slab), gain.reshape(1, -1))
-
-
-def cache_kernel(heads, q_ref, k_ref, v_ref, ok_ref, num_ref, st_ref):
-    ok = ok_ref[...] > 0.0
-    st_ref[...] = jnp.zeros_like(st_ref)
-    for i in range(GROUP):
-        keys = k_ref[0, :, i * HD : (i + 1) * HD]
-        values = v_ref[0, :, i * HD : (i + 1) * HD]
-        scores = jnp.dot(keys, q_ref[i], preferred_element_type=jnp.float32) * HD ** (-0.5)
-        scores = jnp.where(ok, scores, NEG_LARGE)
-        highest = jnp.max(scores, axis=0, keepdims=True)
-        weights = jnp.where(ok, jnp.exp(scores - highest), 0.0)
-        num = lax.dot_general(
-            values,
-            weights.astype(jnp.bfloat16),
-            (((0,), (0,)), ((), ())),
-            preferred_element_type=jnp.float32,
-        )
-        num_ref[i] = num.astype(jnp.bfloat16)
-        slab, row = i // heads, i % heads
-        st_ref[slab, row : row + 1, :] = highest
-        st_ref[slab, GROUP + row : GROUP + row + 1, :] = jnp.sum(weights, axis=0, keepdims=True)
-
-
-def cache_attention(heads, query, keys, values, usable):
-    block = keys.shape[1]
-    cols = GROUP * HD
-    kv = pl.BlockSpec((1, block, cols), lambda i: (0, 0, i))
-    return pl.pallas_call(
-        functools.partial(cache_kernel, heads),
-        grid=(HEADS // GROUP,),
-        in_specs=[
-            pl.BlockSpec((GROUP, HD, SPAN), lambda i: (i, 0, 0)),
-            kv,
-            kv,
-            pl.BlockSpec((block, SPAN), lambda i: (0, 0)),
-        ],
-        out_specs=[
-            pl.BlockSpec((GROUP, HD, SPAN), lambda i: (i, 0, 0)),
-            pl.BlockSpec((GROUP // heads, 2 * GROUP, SPAN), lambda i: (i, 0, 0)),
-        ],
-        out_shape=[
-            jax.ShapeDtypeStruct((HEADS, HD, SPAN), jnp.bfloat16),
-            jax.ShapeDtypeStruct((HEADS // heads, 2 * GROUP, SPAN), jnp.float32),
-        ],
-        compiler_params=params(),
-        name="cache_attention",
-    )(query, keys, values, usable)
 
 
 def body(
@@ -557,21 +649,15 @@
     )
     new_keys = keys_turned.T
     new_values = values_turned.T
-    query_all = query_all.reshape(HEADS, HD, SPAN)
+    query_all = query_all.reshape(wide, heads, HD, SPAN)
     query_turned = query_turned.reshape(heads, HD, SPAN)
 
     block_len = key_cache.shape[1]
     positions = wide_index * block_len + jnp.arange(block_len)
     usable = ((positions < cache_lengths[0]) & (slot_mask[0] == 1)).astype(jnp.float32)
     usable = jnp.broadcast_to(usable[:, None], (block_len, SPAN))
-    num, stats = cache_attention(heads, query_all, key_cache, value_cache, usable)
-    cache_num, cache_stats = reduce_scatter(
-        grid,
-        1,
-        softmax_join,
-        [num.reshape(wide, heads, HD, SPAN), stats],
-        [jnp.float32, jnp.float32],
-        3,
+    cache_num, cache_stats = cache_attention(
+        grid, heads, query_all, key_cache, value_cache, usable, 3
     )
 
     span_count = span_counts[0]
@@ -612,12 +698,11 @@
     both = jnp.einsum("td,cfd->ctf", every_row, gate_up, preferred_element_type=jnp.float32)
     hidden = (jax.nn.silu(both[0]) * both[1]).astype(jnp.bfloat16)
     mlp_part = jnp.dot(hidden, down_weight, preferred_element_type=jnp.float32)
-    (hidden_out,) = reduce_scatter(
+    hidden_out = reduce_scatter(
         grid,
         reqs,
-        add_join,
-        [mlp_part.astype(jnp.bfloat16).reshape(reqs * wide, rows, -1)],
-        [jnp.bfloat16],
+        mlp_part.astype(jnp.bfloat16).reshape(reqs * wide, rows, -1),
+        jnp.bfloat16,
         6,
     )
     return (hidden_out, attention, new_keys, new_values)

time: 171 us -> 149 us (0.87)
  Pallas kernels: 153 us -> 133 us
  local copies, waits for them, and re-layouts: 7.5 us -> 4.8 us
    pallas_call x3 -> x2, Pallas kernels: 63.8 us -> 45.2 us  [the longest x1 25.7 us: cache_attention(): pl.pallas_call(functools.partial(cache_kernel, grid, heads), in_specs=[vm...]
    unnamed x25 -> x15, local copies, waits for them, and re-layouts: 6.32 us -> 2.92 us
where the time goes in v3:
time: 149 us; the launch traced here: 148 us
  Pallas kernels  133 us (89%)
  local copies, waits for them, and re-layouts  4.8 us (3%)
  matrix products  4.12 us (3%)
  other arithmetic  3.65 us (2%)
  between operations  2.45 us (2%)
    pallas_call x1, Pallas kernels, project(): pl.pallas_call(functools.partial(project_kernel, grid, window, chunk), ou...  55.8 us
    pallas_call x1, Pallas kernels, middle(): pl.pallas_call(functools.partial(middle_kernel, grid), out_shape=jax.Shap...  32.4 us
    pallas_call x1, Pallas kernels, cache_attention(): pl.pallas_call(functools.partial(cache_kernel, grid, heads), in_specs=[vm...  25.7 us
    pallas_call x1, Pallas kernels, reduce_scatter(): pl.pallas_call(functools.partial(reduce_kernel, grid, reqs), out_shape=ja...  19.5 us

profile of v3, /device:TPU:0, one launch (start us, length us, event | category | flops | bytes accessed | tf_op | source)
XLA Modules:
  0.0 148.5 jit_solution(16689235154820592349)
XLA Ops:
  0.6 0.0 copy-start
  2.3 0.7 compare_reduce_fusion
  3.0 1.1 fusion.11
  4.1 0.7 reshape.70.gain_ref
  4.8 0.1 fusion.21
  4.9 0.7 convert_element_type.32
  5.6 1.0 fusion.13.x_ref
  6.6 0.1 broadcast_in_dim.30.ok_ref
  6.7 1.0 constant_dynamic-update-slice_fusion.down_ref
  7.8 0.0 copy-start.2
  7.8 1.0 copy-done.2
  8.8 0.0 copy-start.1
  8.8 55.8 %project.1 = (bf16[16,448,128]{2,1,0:T(8,128)(2,1)S(1)}, bf16[448,128]{1,0:T(8,128)(2,1)S(1)}, bf16[448,128]{1,0:T(8,128)(2,1)S(1)}, bf16[448,128]{1,0:T(8,128)(2,1)S(1)}) custom-call(bf16[8,7168]{1,0:T(8,128)(2,1)S(1)} %fusion.13.x_ref, bf16[1344,7168]{1,0:T(8,128)(2,1)} %bitcast.58, bf16[512,384]{1,0:T(8,128)(2,1)S(1)} %constant_dynamic-update-slice_fusion.down_ref, ...), custom_call_target="tpu_custom_call" | custom-call | tf_op jit(solution)/shard_map/project/pallas_call | solution.py:254
  64.6 0.0 copy-done.1
  64.6 0.0 copy-start.3
  64.6 25.7 %cache_attention.1 = (f32[2,224,128]{2,1,0:T(8,128)S(1)}, f32[8,128]{1,0:T(8,128)S(1)}) custom-call(bf16[16,2,224,128]{3,2,1,0:T(8,128)(2,1)S(1)} %bitcast.51, bf16[1,256,7168]{2,1,0:T(8,128)(2,1)S(1)} %copy-done.1, bf16[1,256,7168]{2,1,0:T(8,128)(2,1)} %v_hbm.1, f32[256,128]{1,0:T(8,128)S(1)} %broadcast_in_dim.30.ok_ref), custom_call_target="tpu_custom_call" | custom-call | tf_op jit(solution)/shard_map/cache_attention/pallas_call | solution.py:569
  90.3 0.2 fusion.30
  90.6 0.2 fusion.7
  90.8 0.0 copy-start.4
  90.8 0.0 copy-done.3
  90.8 0.0 copy-start.5
  90.9 0.7 convolution_convert_fusion.1
  91.5 32.4 %middle.1 = bf16[32,8,3584]{2,1,0:T(8,128)(2,1)S(1)} custom-call(bf16[1,4,2,2,8,3584]{5,4,3,2,1,0:T(8,128)(2,1)S(1)} %bitcast.50, bf16[1,3584]{1,0:T(2,128)(2,1)S(1)} %reshape.70.gain_ref), custom_call_target="tpu_custom_call" | custom-call | tf_op jit(solution)/shard_map/middle/pallas_call | solution.py:607
  124.0 0.0 copy-done.4
  124.0 0.0 copy-done.5
  124.0 1.8 %fusion.2 = f32[2,256,448]{1,2,0:T(8,128)S(1)} fusion(bf16[2,448,3584]{2,1,0:T(8,128)(2,1)S(1)} %copy-done.5, bf16[32,8,3584]{2,1,0:T(8,128)(2,1)S(1)} %middle.1), kind=kOutput, calls=%fused_computation.4 | convolution fusion | flops 1644167168 | bytes 9175040 | tf_op jit(solution)/shard_map/td,cfd->ctf/dot_general | solution.py:698
  125.8 0.0 copy-done
  125.9 1.2 convolution_convert_fusion
  127.0 19.5 %reduce6.1 = bf16[8,3584]{1,0:T(8,128)(2,1)S(1)} custom-call(bf16[2,4,2,2,8,3584]{5,4,3,2,1,0:T(8,128)(2,1)S(1)} %bitcast.49), custom_call_target="tpu_custom_call" | custom-call | tf_op jit(solution)/shard_map/reduce6/pallas_call | solution.py:493
  146.6 0.6 copy.24
  147.2 0.6 copy.25
  147.8 0.6 copy.26
  (6 shorter events, 0.1 us)
Async XLA Ops:
  0.6 125.2 %copy-start = (bf16[448,3584]{1,0:T(8,128)(2,1)S(1)}, bf16[448,3584]{1,0:T(8,128)(2,1)}, u32[]{:S(2)}) copy-start(bf16[448,3584]{1,0:T(8,128)(2,1)} %param.22) | copy-start | bytes 9633796
  7.8 1.0 copy-start.2
  8.8 55.8 %copy-start.1 = (bf16[1,256,7168]{2,1,0:T(8,128)(2,1)S(1)}, bf16[1,256,7168]{2,1,0:T(8,128)(2,1)}, u32[]{:S(2)}) copy-start(bf16[1,256,7168]{2,1,0:T(8,128)(2,1)} %k_hbm.1) | copy-start | bytes 11010052
  64.6 26.2 %copy-start.3 = (bf16[448,3584]{1,0:T(8,128)(2,1)S(1)}, bf16[448,3584]{1,0:T(8,128)(2,1)}, u32[]{:S(2)}) copy-start(bf16[448,3584]{1,0:T(8,128)(2,1)} %param.19) | copy-start | bytes 9633796
  90.8 33.1 %copy-start.4 = (bf16[2,224,128]{2,1,0:T(8,128)(2,1)}, bf16[2,224,128]{2,1,0:T(8,128)(2,1)S(1)}, u32[]{:S(2)}) copy-start(bf16[2,224,128]{2,1,0:T(8,128)(2,1)S(1)} %fusion.7) | copy-start | bytes 344068
  90.8 33.1 %copy-start.5 = (bf16[2,448,3584]{2,1,0:T(8,128)(2,1)S(1)}, bf16[2,448,3584]{2,1,0:T(8,128)(2,1)}, u32[]{:S(2)}) copy-start(bf16[2,448,3584]{2,1,0:T(8,128)(2,1)} %param.21) | copy-start | bytes 19267588

commit v4 on v3

--- a/solution.py
+++ b/solution.py
@@ -84,48 +84,71 @@
 
 
 def spread(grid, me, order, x_ref, o_ref, send, recv, local):
+    a, A = me["a"], grid.size["a"]
+    rest = order[1:]
+
     def slot(place):
         at = grid.on_wide(place)
         return place["r"] * grid.wide + at if "r" in order else at
 
+    def guarded(cond, action):
+        if cond is None:
+            action()
+        else:
+            pl.when(cond)(action)
+
     own = pltpu.make_async_copy(x_ref, o_ref.at[slot(me)], local)
     own.start()
-    items = [((0,) * len(order), -1)]
-    for k, axis in enumerate(order):
-        items += [
+    hops = [((0,) * len(rest), -1)]
+    for k, axis in enumerate(rest):
+        hops += [
             (steps[:k] + (s,) + steps[k + 1 :], k)
-            for steps, _ in list(items)
+            for steps, _ in list(hops)
             for s in range(1, grid.size[axis])
         ]
-    items.sort(key=lambda item: (sum(1 for s in item[0] if s), item[1]))
+    lines = [(0, 0)] + [(d, sign) for d in range(1, A) for sign in (-1, 1)]
+    items = [(d, sign, steps, stage) for d, sign in lines for steps, stage in hops]
+    items.sort(key=lambda item: (item[0] + sum(1 for s in item[2] if s), item[3]))
     sends = []
-    for steps, stage in items:
-        place = grid.moved(me, **dict(zip(order, steps)))
+    for d, sign, steps, stage in items:
+        there = None if d == 0 else (a >= d if sign < 0 else a + d < A)
+        place = dict(grid.moved(me, **dict(zip(rest, steps))))
+        place["a"] = (a + sign * d + A) % A
         here = o_ref.at[slot(place)]
-        if stage >= 0:
-            remote(x_ref, here, send.at[0], recv.at[slot(place)], grid.device(me)).wait_recv()
-        source = here if stage >= 0 else x_ref
-        for k in range(stage + 1, len(order)):
-            for s in range(1, grid.size[order[k]]):
-                copy = remote(
-                    source,
-                    here,
-                    send.at[len(sends)],
-                    recv.at[slot(place)],
-                    grid.device(grid.moved(me, **{order[k]: s})),
-                )
-                copy.start()
-                sends.append(copy)
+        is_own = d == 0 and stage < 0
+        source = x_ref if is_own else here
+        made = []
+
+        def add(device, cond):
+            copy = remote(source, here, send.at[len(sends)], recv.at[slot(place)], device)
+            made.append((copy, cond))
+            sends.append((copy, cond))
+
+        if stage < 0:
+            for way in (1, -1):
+                if d == 0 or way == -sign:
+                    room = a + 1 < A if way > 0 else a > 0
+                    cond = room if there is None else jnp.logical_and(there, room)
+                    add(grid.device(dict(me, a=(a + way + A) % A)), cond)
+        for k in range(stage + 1, len(rest)):
+            for s in range(1, grid.size[rest[k]]):
+                add(grid.device(grid.moved(me, **{rest[k]: s})), there)
+        if not is_own:
+            landing = remote(x_ref, here, send.at[0], recv.at[slot(place)], grid.device(me))
+            guarded(there, landing.wait_recv)
+        for copy, cond in made:
+            guarded(cond, copy.start)
     own.wait()
-    for copy in sends:
-        copy.wait_send()
+    for copy, cond in sends:
+        guarded(cond, copy.wait_send)
 
 
 def project_kernel(
     grid,
     window,
     chunk,
-    x_ref,
+    tokens_ref,
+    gain_ref,
     w_hbm,
     down_ref,
     up_ref,
@@ -142,6 +165,7 @@
     t_ref,
     low_ref,
     q_own,
+    x_ref,
     w_sems,
     s1,
     r1,
@@ -154,7 +178,7 @@
     order = ("a", "b", "c")
     n = grid.wide
     at = grid.on_wide(me)
-    rows = x_ref.shape[0]
+    rows = tokens_ref.shape[0]
     width = q_ref.shape[0]
     steps = 3 * width // chunk
 
@@ -162,11 +186,12 @@
         part = pl.ds(i * chunk, chunk)
         return pltpu.make_async_copy(w_hbm.at[part], w_ref.at[part], w_sems.at[i])
 
-    for i in range(steps):
-        load(i).start()
     barrier = pltpu.get_barrier_semaphore()
     for d in range(1, n):
         pl.semaphore_signal(barrier, inc=1, device_id=(me["r"], (at + d) % n), device_id_type=MESH)
+    for i in range(steps):
+        load(i).start()
+    x_ref[...] = rms_scale(tokens_ref[...], gain_ref[...])
     pl.semaphore_wait(barrier, n - 1)
     spread(grid, me, order, x_ref, xs, s1, r1, local.at[0])
 
@@ -237,9 +262,9 @@
         copy.wait_send()
 
 
-def project(grid, normed, qkv_weight, adapter_down, adapter_up, collective_id):
+def project(grid, tokens, gain, qkv_weight, adapter_down, adapter_up, collective_id):
     n = grid.wide
-    rows = normed.shape[0]
+    rows = tokens.shape[0]
     width = qkv_weight.shape[2]
     window = -(-(width + 128 - math.gcd(width, 128)) // 128) * 128
     shift = lax.axis_index("wide") * width % 128
@@ -254,7 +279,7 @@
     return pl.pallas_call(
         functools.partial(project_kernel, grid, window, chunk),
         out_shape=[jax.ShapeDtypeStruct((n, width, SPAN), jnp.bfloat16), turned, turned, turned],
-        in_specs=[vmem, pl.BlockSpec(memory_space=pl.ANY), vmem, vmem],
+        in_specs=[vmem, vmem, pl.BlockSpec(memory_space=pl.ANY), vmem, vmem],
         out_specs=[vmem] * 4,
         scratch_shapes=[
             pltpu.VMEM((3 * width, D), jnp.bfloat16),
@@ -266,17 +291,18 @@
             pltpu.VMEM((rows, 3 * RANK), jnp.bfloat16),
             pltpu.VMEM((n, rows, 3 * RANK), jnp.bfloat16),
             pltpu.VMEM((width, SPAN), jnp.bfloat16),
+            pltpu.VMEM((rows, D), jnp.bfloat16),
             dma((3 * width // chunk,)),
+            dma((2 * n + 2,)),
             dma((n,)),
-            dma((n,)),
-            dma((n,)),
+            dma((2 * n + 2,)),
             dma((n,)),
             dma((2,)),
             dma((4, n)),
         ],
         compiler_params=params(collective_id),
         name="project",
-    )(normed, weight, down, adapter_up.transpose(0, 2, 1))
+    )(tokens, gain.reshape(1, -1), weight, down, adapter_up.transpose(0, 2, 1))
 
 
 def add_join(first, second):
@@ -612,7 +638,7 @@
         scratch_shapes=[pltpu.VMEM(slab, jnp.bfloat16)]
         + reduce_scratch(grid, 1, [(slab, jnp.bfloat16)])
         + [
-            pltpu.SemaphoreType.DMA((slots,)),
+            pltpu.SemaphoreType.DMA((2 * slots + 2,)),
             pltpu.SemaphoreType.DMA((slots,)),
             pltpu.SemaphoreType.DMA,
         ],
@@ -643,9 +669,8 @@
     width = qkv_weight.shape[2]
     heads = width // HD
     wide_index = lax.axis_index("wide")
-    normed = rms_scale(tokens, attn_gain)
     query_all, query_turned, keys_turned, values_turned = project(
-        grid, normed, qkv_weight, adapter_down, adapter_up, 0
+        grid, tokens, attn_gain, qkv_weight, adapter_down, adapter_up, 0
     )
     new_keys = keys_turned.T
     new_values = values_turned.T

time: 149 us -> 140 us (0.940)
  Pallas kernels: 133 us -> 126 us
  other arithmetic: 3.65 us -> 0.86 us
  local copies, waits for them, and re-layouts: 4.8 us -> 6.43 us
    pallas_call x1, Pallas kernels: 25.7 us -> 21.7 us  [cache_attention(): pl.pallas_call(functools.partial(cache_kernel, grid, heads), in_specs=[vm...]
    pallas_call x1, Pallas kernels: 55.8 us -> 52.3 us  [project(): pl.pallas_call(functools.partial(project_kernel, grid, window, chunk), ou...]
    convert_element_type x2 -> x0, other arithmetic: 1.71 us -> none  [the longest x1 0.99 us: rms_scale(): (widened * lax.rsqrt(meansq + EPSILON) * gains.astype(jnp.float32)).astyp...]
    unnamed x15 -> x17, local copies, waits for them, and re-layouts: 2.92 us -> 3.82 us
where the time goes in v4:
time: 140 us
  Pallas kernels  126 us (90%)
  local copies, waits for them, and re-layouts  6.43 us (5%)
  matrix products  4.12 us (3%)
  between operations  2.45 us (2%)
    pallas_call x1, Pallas kernels, project(): pl.pallas_call(functools.partial(project_kernel, grid, window, chunk), ou...  52.3 us
    pallas_call x1, Pallas kernels, middle(): pl.pallas_call(functools.partial(middle_kernel, grid), out_shape=jax.Shap...  33.8 us
    pallas_call x1, Pallas kernels, cache_attention(): pl.pallas_call(functools.partial(cache_kernel, grid, heads), in_specs=[vm...  21.7 us
    pallas_call x1, Pallas kernels, reduce_scatter(): pl.pallas_call(functools.partial(reduce_kernel, grid, reqs), out_shape=ja...  18.5 us
    unnamed x17, local copies, waits for them, and re-layouts  3.82 us

profile of v4, /device:TPU:0, one launch (start us, length us, event | category | flops | bytes accessed | tf_op | source)
XLA Modules:
  0.0 140.1 jit_solution(17267860563283851724)
XLA Ops:
  0.6 0.0 copy-start
  2.3 0.7 compare_reduce_fusion
  3.0 0.7 reshape.65.gain_ref
  3.7 0.1 fusion.18
  3.8 0.7 reshape.58.gain_ref
  4.5 0.1 broadcast_in_dim.28.ok_ref
  4.7 1.0 constant_dynamic-update-slice_fusion.down_ref
  5.7 0.0 copy-start.2
  5.7 1.0 copy-done.2
  6.7 0.0 copy-start.3
  6.7 0.9 copy-done.3
  7.6 0.0 copy-start.1
  7.6 52.3 %project.1 = (bf16[16,448,128]{2,1,0:T(8,128)(2,1)S(1)}, bf16[448,128]{1,0:T(8,128)(2,1)S(1)}, bf16[448,128]{1,0:T(8,128)(2,1)S(1)}, bf16[448,128]{1,0:T(8,128)(2,1)S(1)}) custom-call(bf16[8,7168]{1,0:T(8,128)(2,1)S(1)} %copy-done.3, bf16[1,7168]{1,0:T(2,128)(2,1)S(1)} %reshape.58.gain_ref, bf16[1344,7168]{1,0:T(8,128)(2,1)} %bitcast.58, ...), custom_call_target="tpu_custom_call" | custom-call | tf_op jit(solution)/shard_map/project/pallas_call | solution.py:279
  59.9 0.0 copy-done.1
  59.9 0.0 copy-start.4
  59.9 21.7 %cache_attention.1 = (f32[2,224,128]{2,1,0:T(8,128)S(1)}, f32[8,128]{1,0:T(8,128)S(1)}) custom-call(bf16[16,2,224,128]{3,2,1,0:T(8,128)(2,1)S(1)} %bitcast.51, bf16[1,256,7168]{2,1,0:T(8,128)(2,1)S(1)} %copy-done.1, bf16[1,256,7168]{2,1,0:T(8,128)(2,1)} %v_hbm.1, f32[256,128]{1,0:T(8,128)S(1)} %broadcast_in_dim.28.ok_ref), custom_call_target="tpu_custom_call" | custom-call | tf_op jit(solution)/shard_map/cache_attention/pallas_call | solution.py:595
  81.6 0.2 fusion.27
  81.9 0.2 fusion.7
  82.1 0.0 copy-start.5
  82.1 0.0 copy-done.4
  82.1 0.0 copy-start.6
  82.1 0.7 convolution_convert_fusion.1
  82.8 33.8 %middle.1 = bf16[32,8,3584]{2,1,0:T(8,128)(2,1)S(1)} custom-call(bf16[1,4,2,2,8,3584]{5,4,3,2,1,0:T(8,128)(2,1)S(1)} %bitcast.50, bf16[1,3584]{1,0:T(2,128)(2,1)S(1)} %reshape.65.gain_ref), custom_call_target="tpu_custom_call" | custom-call | tf_op jit(solution)/shard_map/middle/pallas_call | solution.py:633
  116.6 0.0 copy-done.5
  116.6 0.0 copy-done.6
  116.6 1.8 %fusion.2 = f32[2,256,448]{1,2,0:T(8,128)S(1)} fusion(bf16[2,448,3584]{2,1,0:T(8,128)(2,1)S(1)} %copy-done.6, bf16[32,8,3584]{2,1,0:T(8,128)(2,1)S(1)} %middle.1), kind=kOutput, calls=%fused_computation.4 | convolution fusion | flops 1644167168 | bytes 9175040 | tf_op jit(solution)/shard_map/td,cfd->ctf/dot_general | solution.py:723
  118.5 0.0 copy-done
  118.5 1.2 convolution_convert_fusion
  119.6 18.5 %reduce6.1 = bf16[8,3584]{1,0:T(8,128)(2,1)S(1)} custom-call(bf16[2,4,2,2,8,3584]{5,4,3,2,1,0:T(8,128)(2,1)S(1)} %bitcast.49), custom_call_target="tpu_custom_call" | custom-call | tf_op jit(solution)/shard_map/reduce6/pallas_call | solution.py:519
  138.2 0.6 copy.24
  138.8 0.6 copy.25
  139.4 0.6 copy.26
  (5 shorter events, 0.1 us)
Async XLA Ops:
  0.6 117.8 %copy-start = (bf16[448,3584]{1,0:T(8,128)(2,1)S(1)}, bf16[448,3584]{1,0:T(8,128)(2,1)}, u32[]{:S(2)}) copy-start(bf16[448,3584]{1,0:T(8,128)(2,1)} %param.22) | copy-start | bytes 9633796
  5.7 1.0 copy-start.2
  6.7 0.9 copy-start.3
  7.6 52.3 %copy-start.1 = (bf16[1,256,7168]{2,1,0:T(8,128)(2,1)S(1)}, bf16[1,256,7168]{2,1,0:T(8,128)(2,1)}, u32[]{:S(2)}) copy-start(bf16[1,256,7168]{2,1,0:T(8,128)(2,1)} %k_hbm.1) | copy-start | bytes 11010052
  59.9 22.2 %copy-start.4 = (bf16[448,3584]{1,0:T(8,128)(2,1)S(1)}, bf16[448,3584]{1,0:T(8,128)(2,1)}, u32[]{:S(2)}) copy-start(bf16[448,3584]{1,0:T(8,128)(2,1)} %param.19) | copy-start | bytes 9633796
  82.1 34.5 %copy-start.5 = (bf16[2,224,128]{2,1,0:T(8,128)(2,1)}, bf16[2,224,128]{2,1,0:T(8,128)(2,1)S(1)}, u32[]{:S(2)}) copy-start(bf16[2,224,128]{2,1,0:T(8,128)(2,1)S(1)} %fusion.7) | copy-start | bytes 344068
  82.1 34.5 %copy-start.6 = (bf16[2,448,3584]{2,1,0:T(8,128)(2,1)S(1)}, bf16[2,448,3584]{2,1,0:T(8,128)(2,1)}, u32[]{:S(2)}) copy-start(bf16[2,448,3584]{2,1,0:T(8,128)(2,1)} %param.21) | copy-start | bytes 19267588
